TPU v7x, 32 devices: a whole 2x2x4 slice. The times are simulated.
32 devices in a mesh: dp: 8 (over y, x, core), tensor: 4 (over z).
Axes of the slice: x: 2, y: 2, z: 4, core: 2. Of those that a mesh axis runs over, the one named last changes fastest.
Arguments:
- tokens: bfloat16 [8, 1032, 1024], P('dp', 'tensor'), may hold values from -6 to 6
- cotangent: bfloat16 [8, 1032, 1024], P('dp', 'tensor'), may hold values from -6 to 6
- w_qkv: bfloat16 [3, 1024, 1024], P(None, 'dp', 'tensor'), may hold values from -0.1875 to 0.1875
- w_o: bfloat16 [1024, 1024], P('tensor', 'dp'), may hold values from -0.1875 to 0.1875
- w_gu: bfloat16 [2, 1024, 2736], P(None, 'dp', 'tensor'), may hold values from -0.1875 to 0.1875
- w_down: bfloat16 [2736, 1024], P('tensor', 'dp'), may hold values from -0.109375 to 0.109375
- norm_params: float32 [6, 1024], replicated, may hold values from -1.5 to 1.65, as said below
- head_params: float32 [4, 1024], replicated, may hold values from -1.5 to 1.65, as said below
- ffn_params: float32 [4, 2736], replicated, may hold values from -1.5 to 1.65, as said below
- token_mask: int32 [8, 1032], P('dp'), may hold values from 0 to 1, as said below
- empty_flag: int32 [8], P('dp'), may hold values from 0 to 1, as said below
- coords: int32 [8, 2, 1032], P('dp'), may hold values from 0 to 31, as said below
Outputs:
- layer_out: bfloat16 [8, 1032, 1024], P('dp', 'tensor')
- d_tokens: float32 [8, 1032, 1024], P('dp', 'tensor')
- d_w_qkv: float32 [3, 1024, 1024], P(None, 'dp', 'tensor')
- d_w_o: float32 [1024, 1024], P('tensor', 'dp')
- d_w_gu: float32 [2, 1024, 2736], P(None, 'dp', 'tensor')
- d_w_down: float32 [2736, 1024], P('tensor', 'dp')
- d_norm_params: float32 [6, 1024], replicated
- d_head_params: float32 [4, 1024], replicated
- d_ffn_params: float32 [4, 2736], replicated
Inputs may be any that keep to these rules, and one draw needn't show every extreme that they name: `token_mask`: in every image slot 0 (the class token) is 1, the patch slots 1 to 1024 are 1 or 0, and the later slots are 0. `empty_flag`: at least one image is flagged. `coords`: row 0 holds grid rows, row 1 grid columns; the patch slots of an image hold every position of the 32 x 32 grid once, in an order drawn per image; slot 0 and the later slots hold 0. `norm_params`: gain rows lie within 0.6 to 1.65, the other rows within -1.5 to 1.5. `head_params`: gain rows lie within 0.6 to 1.65, the other rows within -1.5 to 1.5. `ffn_params`: gain rows lie within 0.6 to 1.65, the other rows within -1.5 to 1.5.
All inputs are finite; a program needn't handle non-finite values.
Results may differ from a plain program's by a relative error of at most 0.015.
Values may be sent and summed in bfloat16 or wider, within the bound.
No kernel may reach another device: no remote copies, remote signals or barrier semaphores. Data moves between devices by JAX's collectives and lax.ppermute only.
A program may use at most 192 MiB of HBM per device.

v0:
```python
import functools
import math

import jax
import jax.numpy as jnp
from jax import lax
from jax.experimental import pallas as pl
from jax.experimental.pallas import tpu as pltpu
from jax.sharding import PartitionSpec as P

FF = 2730
HD = 64
FF_PAD = 2736
GRID_SIDE = 32
LANES = 128
EPS = 1e-06
VMEM_LIMIT = 44 * 2**20
COST_SCALE = 4.0
BF = jnp.bfloat16
F32 = jnp.float32
NT = (((1,), (1,)), ((), ()))
TN = (((0,), (0,)), ((), ()))


def ring_up(value, size):
    return lax.ppermute(value, "tensor", [(j, (j + 1) % size) for j in range(size)])


def ring_down(value, size):
    return lax.ppermute(value, "tensor", [(j, (j - 1) % size) for j in range(size)])


def ring_offsets(size):
    ups = size // 2
    return [0] + [-s for s in range(1, ups + 1)] + [s for s in range(1, size - ups)]


def gather_rest(own, first, size, late=None):
    ups = size // 2
    downs = size - 1 - ups
    upper, lower = first[:1], first[1:]
    for s in range(1, ups):
        up_now = upper[-1] if late is None else after(upper[-1], late)
        upper.append(ring_up(up_now, size))
        if s < downs:
            down_now = lower[-1] if late is None else after(lower[-1], late)
            lower.append(ring_down(down_now, size))
    return [own] + upper + lower


def ring_gather(own, size):
    return gather_rest(own, [ring_up(own, size), ring_down(own, size)], size)


def after(value, *others):
    return lax.optimization_barrier((value,) + others)[0]


def sum_shifts(value, size):
    total = value
    for s in range(1, size):
        total = total + lax.ppermute(
            value, "tensor", [(j, (j + s) % size) for j in range(size)]
        )
    return total


def gather_small(value, size):
    return [value] + [
        lax.ppermute(value, "tensor", [(j, (j + s) % size) for j in range(size)])
        for s in range(1, size)
    ]


def sum_alike(terms):
    while len(terms) > 1 and len(terms) % 2 == 0:
        half = len(terms) // 2
        terms = [terms[s] + terms[s + half] for s in range(half)]
    return functools.reduce(jnp.add, terms)


def swap_sum(blocks, size):
    index = lax.axis_index("tensor")

    def block_for(s):
        return lax.dynamic_index_in_dim(blocks, (index + s) % size, 0, keepdims=False)

    total = block_for(0).astype(F32)
    for s in range(1, size):
        came = lax.ppermute(block_for(s), "tensor", [(j, (j + s) % size) for j in range(size)])
        total = total + came.astype(F32)
    return total


def add_low(left, right):
    return (left.astype(F32) + right.astype(F32)).astype(BF)


def scatter_first(pieces, size):
    place = {offset % size: at for at, offset in enumerate(ring_offsets(size))}
    ups = size // 2
    arrived = []
    if size > 1:
        arrived.append(ring_up(pieces[place[ups % size]], size))
    if ups == size - 1 - ups:
        arrived.append(ring_down(pieces[place[-ups % size]], size))
    elif size > 2:
        arrived.append(ring_down(pieces[place[(1 - ups) % size]], size))
    return arrived


def scatter_rest(pieces, arrived, size, sent=None):
    place = {offset % size: at for at, offset in enumerate(ring_offsets(size))}
    ups = size // 2
    downs = size - 1 - ups
    up_now = arrived[0]
    for s in range(ups - 1, 0, -1):
        up_now = add_low(up_now, pieces[place[s]])
        if sent is not None:
            sent.append(up_now)
        up_now = ring_up(up_now, size)
    terms = [pieces[0], up_now]
    if downs:
        down_now = arrived[1]
        for s in range(downs - 1, 0, -1):
            down_now = ring_down(add_low(down_now, pieces[place[-s % size]]), size)
        terms.append(down_now)
    return terms


def dp_bits(size):
    bits = []
    step = 2
    while step < size:
        bits.append(step)
        step *= 2
    return bits + ([1] if size > 1 else [])


def flip(value, bit, size):
    return lax.ppermute(value, "dp", [(j, j ^ bit) for j in range(size)])


def dp_gather(block, size, late=None):
    stacked = block[None]
    bits = dp_bits(size)
    for bit in bits[:-1]:
        other = flip(stacked, bit, size)
        if late is not None and bit == bits[-2]:
            other = after(other, late)
        stacked = jnp.concatenate([stacked, other], axis=0)
    return [stacked] + [flip(stacked, bit, size) for bit in bits[-1:]]


def dp_order(size):
    order = [0]
    for bit in dp_bits(size):
        order = order + [at ^ bit for at in order]
    return jnp.array(order, jnp.int32) ^ lax.axis_index("dp")


def pair_sum(halves, size):
    kept, away = halves
    return add_low(kept, flip(away, 1, size))


def dp_scatter(merged, size):
    groups = [[j for j in range(size) if j % 2 == c] for c in range(2)]
    return lax.all_to_all(
        merged, "dp", split_axis=0, concat_axis=0, tiled=True, axis_index_groups=groups
    )


def sum_parts(parts):
    return jnp.sum(parts.astype(F32), axis=0)


def sum_over(value, axis, size):
    copies = jnp.broadcast_to(value[None], (size,) + value.shape)
    return jnp.sum(lax.all_to_all(copies, axis, split_axis=0, concat_axis=0, tiled=True), axis=0)


def whole(shape):
    return pl.BlockSpec(shape, lambda *_: (0,) * len(shape))


def lead(shape):
    return pl.BlockSpec((1,) + shape, lambda s, *_: (s,) + (0,) * len(shape))


def placed(shape):
    return pl.BlockSpec((1,) + shape, lambda s, place, *_: (place[s],) + (0,) * len(shape))


def ordered(shape):
    return pl.BlockSpec(
        (1,) + shape, lambda s, place, order: (order[place[s]],) + (0,) * len(shape)
    )


def call(
    body, args, specs, outs, out_specs, grid, scratch=(), prefetch=0, held=(), us=1.0
):
    first_held = len(args)
    args = tuple(args) + tuple(held)
    specs = list(specs) + [pl.BlockSpec(memory_space=pl.ANY)] * len(held)
    return pl.pallas_call(
        body,
        out_shape=outs,
        grid_spec=pltpu.PrefetchScalarGridSpec(
            num_scalar_prefetch=prefetch,
            grid=grid,
            in_specs=specs,
            out_specs=out_specs,
            scratch_shapes=list(scratch),
        ),
        input_output_aliases={first_held + at: at for at in range(len(held))},
        compiler_params=pltpu.CompilerParams(vmem_limit_bytes=VMEM_LIMIT),
        cost_estimate=pl.CostEstimate(
            flops=int(us * COST_SCALE * 1e9), bytes_accessed=1, transcendentals=0
        ),
    )(*args)


def sds(shape, dtype):
    return jax.ShapeDtypeStruct(shape, dtype)


def row_stats(rows, count):
    mean = jnp.sum(rows, axis=1, keepdims=True) / count
    power = jnp.sum(rows * rows, axis=1, keepdims=True) / count
    return mean, lax.rsqrt(power - mean * mean + EPS)


def rows_back(upstream, gain, unit, inv, count):
    scaled = upstream * gain
    first = jnp.sum(scaled, axis=1, keepdims=True) / count
    second = jnp.sum(scaled * unit, axis=1, keepdims=True) / count
    return inv * (scaled - first - unit * second)


def down_sum(rows):
    return jnp.sum(rows, axis=0, keepdims=True)


def put_back_body(count, near, *refs):
    in_refs, out_ref = refs[1:-1], refs[-1]
    for at in range(count):

        @pl.when(pl.program_id(0) // near == at)
        def _():
            out_ref[...] = in_refs[at][(0,) * (len(in_refs[at].shape) - len(out_ref.shape))]


def put_back(order, stacks, axis):
    count, near, block = len(stacks), stacks[0].shape[0], stacks[0].shape[1:]
    size = count * near
    shape = tuple(n * size if at == axis else n for at, n in enumerate(block))
    if block[axis] % (LANES if axis == len(block) - 1 else 16):
        stacked = jnp.concatenate(stacks, axis=0)
        placed = jnp.zeros_like(stacked).at[order].set(stacked)
        return jnp.moveaxis(placed, 0, axis).reshape(shape)

    def taken(at):
        return pl.BlockSpec(
            (1,) + block,
            lambda r, order: (jnp.clip(r - at * near, 0, near - 1),) + (0,) * len(block),
        )

    return call(
        functools.partial(put_back_body, count, near),
        (order, *stacks),
        [taken(at) for at in range(count)],
        [sds(shape, stacks[0].dtype)],
        [
            pl.BlockSpec(
                block,
                lambda r, order: tuple(order[r] if at == axis else 0 for at in range(len(block))),
            )
        ],
        (size,),
        prefetch=1,
        us=size * math.prod(block) / 2**19,
    )[0]


def first_norm_body(tokens_ref, norm_ref, normed_ref):
    rows = tokens_ref[...].astype(F32)
    length, width = rows.shape
    mean, inv = row_stats(rows, width)
    normed_ref[:length] = ((rows - mean) * inv * norm_ref[0:1, :] + norm_ref[1:2, :]).astype(BF)
    normed_ref[length:] = jnp.zeros((normed_ref.shape[0] - length, width), BF)


def lay_body(order_ref, *refs):
    out_ref = refs[-1]
    for at, ref in enumerate(refs[:-1]):
        piece = ref[...].astype(F32).T.astype(BF)
        out_ref[order_ref[at]] = piece


def spread(table, width):
    return table if width == LANES else jnp.concatenate([table] * (width // LANES), axis=1)


def turn_pairs(rows):
    width = rows.shape[1]
    even = lax.broadcasted_iota(jnp.int32, (1, width), 1) % 2 == 0
    return jnp.where(even, -pltpu.roll(rows, width - 1, 1), pltpu.roll(rows, 1, 1))


def pick(held, chunk_refs):
    for at, ref in enumerate(chunk_refs):

        @pl.when(pl.program_id(0) == at)
        def _():
            held[...] = ref[...]

    return held[...]


def project_body(count, place_ref, *refs):
    chunk_refs = refs[:count]
    w_ref, head_ref, cos_ref, sin_ref = refs[count : count + 4]
    q_ref, k_ref, v_ref, held = refs[-4:]
    rows = pick(held, chunk_refs)
    width = w_ref.shape[2]
    cosine, sine = spread(cos_ref[...], width), spread(sin_ref[...], width)
    query = jnp.dot(rows, w_ref[0], preferred_element_type=F32) + head_ref[0:1, :]
    key = jnp.dot(rows, w_ref[1], preferred_element_type=F32)
    value = jnp.dot(rows, w_ref[2], preferred_element_type=F32) + head_ref[1:2, :]
    query_low = (query * cosine + turn_pairs(query) * sine).astype(BF)
    q_ref[0] = (query_low.astype(F32) * HD ** (-0.5)).astype(BF)
    k_ref[0] = (key * cosine + turn_pairs(key) * sine).astype(BF)
    v_ref[0] = value.astype(BF)


def head_lanes(width, head):
    lane = lax.broadcasted_iota(jnp.int32, (1, width), 1)
    return (lane >= head * HD) & (lane < (head + 1) * HD)


def attend_body(order_ref, q_ref, k_ref, v_ref, bias_ref, mixed_ref, lse_ref):
    query, keys, values, bias = q_ref[...], k_ref[...], v_ref[...], bias_ref[...]
    length, width = query.shape
    total = jnp.zeros((length, width), F32)
    for head in range(width // HD):
        mine = head_lanes(width, head)
        query_h = jnp.where(mine, query, jnp.zeros_like(query))
        scores = lax.dot_general(query_h, keys, NT, preferred_element_type=F32) + bias
        row_max = jnp.max(scores, axis=1, keepdims=True)
        exp_score = jnp.exp(scores - row_max)
        row_total = jnp.sum(exp_score, axis=1, keepdims=True)
        out = jnp.dot(exp_score.astype(BF), values, preferred_element_type=F32)
        total = jnp.where(mine, out * (1.0 / row_total), total)
        lse_ref[0, head : head + 1, :] = (row_max + jnp.log(row_total)).reshape(1, length)
    rows = mixed_ref.shape[1]
    for part in range(length // rows):
        at = order_ref[pl.program_id(0) * (length // rows) + part]
        mixed_ref[at] = total[part * rows : (part + 1) * rows].astype(BF)


def attend_back_body(
    order_ref,
    q_ref,
    dmix_ref,
    lse_ref,
    k_ref,
    v_ref,
    bias_ref,
    cos_ref,
    sin_ref,
    coss_ref,
    sins_ref,
    dq_ref,
    dk_ref,
    dv_ref,
    sums_ref,
    dk_sum,
    dv_sum,
):
    step = pl.program_id(0)

    @pl.when(step == 0)
    def _():
        dk_sum[...] = jnp.zeros_like(dk_sum)
        dv_sum[...] = jnp.zeros_like(dv_sum)
        sums_ref[...] = jnp.zeros_like(sums_ref)

    query, keys, values, bias = q_ref[...], k_ref[...], v_ref[...], bias_ref[...]
    length, width = query.shape
    rows = dmix_ref.shape[1]
    parts = length // rows
    d_mixed = jnp.concatenate([dmix_ref[order_ref[step * parts + p]] for p in range(parts)], axis=0)
    total = jnp.zeros((length, width), F32)
    for head in range(width // HD):
        mine = head_lanes(width, head)
        zero = jnp.zeros_like(query)
        query_h, d_mixed_h = jnp.where(mine, query, zero), jnp.where(mine, d_mixed, zero)
        scores = lax.dot_general(keys, query_h, NT, preferred_element_type=F32) + bias
        probs = jnp.exp(scores - lse_ref[0, head : head + 1, :])
        d_probs = lax.dot_general(values, d_mixed_h, NT, preferred_element_type=F32)
        d_scores = (probs * (d_probs - down_sum(probs * d_probs))).astype(BF)
        dv_sum[...] += jnp.dot(probs.astype(BF), d_mixed_h, preferred_element_type=F32)
        dk_sum[...] += jnp.dot(d_scores, query_h, preferred_element_type=F32)
        d_query = lax.dot_general(d_scores, keys, TN, preferred_element_type=F32)
        total = jnp.where(mine, d_query, total)
    total = total * HD ** (-0.5)
    cosine, sine = spread(cos_ref[...], width), spread(sin_ref[...], width)
    d_query_pre = (total * cosine - turn_pairs(total) * sine).astype(BF)
    dq_ref[...] = d_query_pre
    sums_ref[0:1, :] += down_sum(d_query_pre.astype(F32))

    @pl.when(step == pl.num_programs(0) - 1)
    def _():
        d_key = dk_sum[...]
        all_cos, all_sin = spread(coss_ref[...], width), spread(sins_ref[...], width)
        d_key_pre = (d_key * all_cos - turn_pairs(d_key) * all_sin).astype(BF)
        dk_ref[...] = d_key_pre
        sums_ref[1:2, :] = down_sum(d_key_pre.astype(F32))
        d_value_pre = dv_sum[...].astype(BF)
        dv_ref[...] = d_value_pre
        sums_ref[2:3, :] = down_sum(d_value_pre.astype(F32))


def mixed_rows(mixed_ref):
    parts = mixed_ref.shape[0]
    return jnp.concatenate([mixed_ref[p] for p in range(parts)], axis=1).astype(F32)


def middle_body(
    mixed_ref, tokens_ref, keep_ref, w_ref, norm_ref, head_ref, inner_ref, middle_ref, normed_ref
):
    mixed = mixed_rows(mixed_ref)
    mean, inv = row_stats(mixed, mixed.shape[1])
    inner = ((mixed - mean) * inv * head_ref[2:3, :] + head_ref[3:4, :]).astype(BF)
    inner_ref[...] = inner
    branch = lax.dot_general(inner, w_ref[...], NT, preferred_element_type=F32)
    branch += norm_ref[4:5, :]
    middle = tokens_ref[...].astype(F32) + keep_ref[...] * branch
    middle_ref[...] = middle
    mean, inv = row_stats(middle, middle.shape[1])
    normed_ref[...] = ((middle - mean) * inv * norm_ref[2:3, :] + norm_ref[3:4, :]).astype(BF)


def sigmoid(gate):
    return 1.0 / (1.0 + jnp.exp(-gate))


def d_ffn_body(count, *refs):
    w_ref, out_refs, held = refs[count], refs[count + 1 : -1], refs[-1]
    out = jnp.dot(pick(held, refs[:count]), w_ref[0], preferred_element_type=F32)
    for at in range(count):

        @pl.when(pl.program_id(0) == at)
        def _():
            out_refs[at][...] = out


def ffn_body(count, place_ref, order_ref, *refs):
    w_gu_ref, ffn_ref, unit_ref = refs[2 * count : 2 * count + 3]
    gate_ref, up_ref, stats_ref, held, d_held = refs[-5:]
    rows = pick(held, refs[:count])
    d_ffn = pick(d_held, refs[count : 2 * count])
    gate = jnp.dot(rows, w_gu_ref[0], preferred_element_type=F32) + ffn_ref[0:1, :]
    up = jnp.dot(rows, w_gu_ref[1], preferred_element_type=F32) + ffn_ref[1:2, :]
    gate_ref[0], up_ref[0] = gate, up
    unit = unit_ref[...]
    hidden = gate * sigmoid(gate) * up
    masked = hidden * unit
    scaled = d_ffn * ffn_ref[2:3, :] * unit
    length = rows.shape[0]
    for at, term in enumerate((masked, masked * hidden, scaled, scaled * hidden)):
        stats_ref[0, at : at + 1, :] = jnp.sum(term, axis=1, keepdims=True).reshape(1, length)


def ffn_back_body(count, place_ref, order_ref, *refs):
    gate_ref, up_ref = refs[:2]
    stats_ref, w_gu_ref, ffn_ref, unit_ref = refs[2 + count : 6 + count]
    low_ref, dgate_ref, dup_ref, sums_ref = refs[-5 - count : -1 - count]
    out_refs = refs[-1 - count : -1]
    d_ffn = pick(refs[-1], refs[2 : 2 + count])
    step = pl.program_id(0)

    @pl.when(step == 0)
    def _():
        sums_ref[...] = jnp.zeros_like(sums_ref)

    gate, up, unit = gate_ref[0], up_ref[0], unit_ref[...]
    gain = ffn_ref[2:3, :]
    stats = stats_ref[0]
    mean = stats[:, 0:1] / FF
    inv = lax.rsqrt(stats[:, 1:2] / FF - mean * mean + EPS)
    first = stats[:, 2:3]
    second = inv * (stats[:, 3:4] - mean * first)
    sig = sigmoid(gate)
    silu = gate * sig
    unit_value = (silu * up - mean) * inv
    low_ref[0] = (unit * (unit_value * gain + ffn_ref[3:4, :])).astype(BF)
    d_hidden = unit * inv * (d_ffn * gain * unit - first / FF - unit_value * (second / FF))
    d_gate = (d_hidden * up * sig * (1.0 + gate * (1.0 - sig))).astype(BF)
    d_up = (d_hidden * silu).astype(BF)
    dgate_ref[0], dup_ref[0] = d_gate, d_up
    d_masked = d_ffn * unit
    sums_ref[0:1, :] += down_sum(d_gate.astype(F32))
    sums_ref[1:2, :] += down_sum(d_up.astype(F32))
    sums_ref[2:3, :] += down_sum(d_masked * unit_value)
    sums_ref[3:4, :] += down_sum(d_masked)
    out = lax.dot_general(d_gate, w_gu_ref[0], NT, preferred_element_type=F32)
    out += lax.dot_general(d_up, w_gu_ref[1], NT, preferred_element_type=F32)
    for at in range(count):

        @pl.when(step == at)
        def _():
            out_refs[at][...] = out.astype(BF)


def down_body(count, low_ref, w_ref, *out_refs):
    out = lax.dot_general(low_ref[0], w_ref[0], NT, preferred_element_type=F32)
    for at in range(count):

        @pl.when(pl.program_id(0) == at)
        def _():
            out_refs[at][...] = out.astype(BF)


def spread_back_body(count, place_ref, dq_ref, dk_ref, dv_ref, w_ref, *out_refs):
    out = lax.dot_general(dq_ref[...], w_ref[0], NT, preferred_element_type=F32)
    out += lax.dot_general(dk_ref[...], w_ref[1], NT, preferred_element_type=F32)
    out += lax.dot_general(dv_ref[...], w_ref[2], NT, preferred_element_type=F32)
    for at in range(count):

        @pl.when(pl.program_id(0) == at)
        def _():
            out_refs[at][...] = out.astype(BF)


def product_body(n_left, sizes, block, parity_ref, *refs):
    lefts, at = [], 0
    for count in n_left:
        lefts.append(jnp.concatenate([ref[...] for ref in refs[at : at + count]], axis=0))
        at += count
    rights = []
    for size in sizes:
        rights.append([ref[...] for ref in refs[at : at + size]])
        at += size
    w_refs = refs[at:-3] if len(refs) - at > 2 else []
    kept_ref, away_ref = refs[at + len(w_refs) : at + len(w_refs) + 2]
    parity = parity_ref[0]
    column, along = 0, 0.0
    for left, group in zip(lefts, rights):
        for right in group:
            out = lax.dot_general(left, right, TN, preferred_element_type=F32)
            width = right.shape[1]
            if w_refs and column < w_refs[0].shape[0] * w_refs[0].shape[2]:
                part = w_refs[0][column // width].astype(F32)
                along = along + jnp.sum(out * part, axis=1, keepdims=True)
            low = out.astype(BF)
            for pair in range(out.shape[0] // (2 * block)):
                first = low[2 * pair * block : (2 * pair + 1) * block]
                second = low[(2 * pair + 1) * block : (2 * pair + 2) * block]
                mine = jnp.where(parity == 0, first, second)
                other = jnp.where(parity == 0, second, first)
                kept_ref[pair, :, column : column + width] = mine
                away_ref[pair, :, column : column + width] = other
            column += width
    if w_refs:
        refs[-1][0] = along.reshape(1, along.shape[0])


def product(lefts, rights, parity, block, weights=None):
    width = lefts[0][0].shape[1]
    step = max(256, 2 * block)
    pairs = step // (2 * block)
    columns = sum(right.shape[1] for group in rights for right in group)
    args = [left for group in lefts for left in group]
    specs = [
        pl.BlockSpec((left.shape[0], step), lambda m, *_: (0, m)) for group in lefts for left in group
    ]
    for group in rights:
        args += group
        specs += [whole(right.shape) for right in group]
    outs = [sds((width // (2 * block), block, columns), BF)] * 2
    out_specs = [pl.BlockSpec((pairs, block, columns), lambda m, *_: (m, 0, 0))] * 2
    if weights is not None:
        args.append(weights)
        specs.append(
            pl.BlockSpec((weights.shape[0], step, weights.shape[2]), lambda m, *_: (0, m, 0))
        )
        outs.append(sds((width // step, 1, step), F32))
        out_specs.append(lead((1, step)))
    return call(
        functools.partial(
            product_body, [len(g) for g in lefts], [len(g) for g in rights], block
        ),
        (parity, *args),
        specs,
        outs,
        out_specs,
        (width // step,),
        prefetch=1,
        us=columns / 250,
    )


def add_terms(term_refs):
    total = term_refs[0][...].astype(F32)
    for ref in term_refs[1:]:
        total += ref[...].astype(F32)
    return total


def middle_back_body(count, *refs):
    upstream = add_terms(refs[:count])
    middle_ref, dy_ref, low_ref, keep_ref, mixed_ref, w_ref, norm_ref, head_ref = refs[
        count : count + 8
    ]
    dmid_ref, dbranch_ref, dmix_ref, sums_ref = refs[count + 8 :]
    middle = middle_ref[...]
    width = middle.shape[1]
    mean, inv = row_stats(middle, width)
    unit = (middle - mean) * inv
    d_middle = dy_ref[...].astype(F32) + rows_back(upstream, norm_ref[2:3, :], unit, inv, width)
    dmid_ref[...] = d_middle
    sums_ref[0:1, :] = down_sum(upstream * unit)
    sums_ref[1:2, :] = down_sum(upstream)
    d_branch = (keep_ref[...] * d_middle).astype(BF)
    dbranch_ref[...] = d_branch
    sums_ref[2:3, :] = down_sum(d_branch.astype(F32))
    sums_ref[3:4, :] = down_sum(low_ref[...].astype(F32))
    d_inner = jnp.dot(d_branch, w_ref[...], preferred_element_type=F32)
    mixed = mixed_rows(mixed_ref)
    mean, inv = row_stats(mixed, width)
    unit = (mixed - mean) * inv
    d_mixed = rows_back(d_inner, head_ref[2:3, :], unit, inv, width).astype(BF)
    part = mixed_ref.shape[2]
    for at in range(mixed_ref.shape[0]):
        dmix_ref[at] = d_mixed[:, at * part : (at + 1) * part]
    sums_ref[4:5, :] = down_sum(d_inner * unit)
    sums_ref[5:6, :] = down_sum(d_inner)
    sums_ref[6:8, :] = jnp.zeros((2, width), F32)


def first_back_body(count, *refs):
    upstream = add_terms(refs[:count])
    tokens_ref, dmid_ref, norm_ref, out_ref = refs[count:]
    rows = tokens_ref[...].astype(F32)
    length, width = rows.shape
    mean, inv = row_stats(rows, width)
    unit = (rows - mean) * inv
    d_in = rows_back(upstream[:length], norm_ref[0:1, :], unit, inv, width)
    out_ref[...] = dmid_ref[:length] + d_in


def layer_out_body(count, *refs):
    branch = add_terms(refs[:count])
    middle_ref, keep_ref, norm_ref, out_ref = refs[count:]
    out = middle_ref[...] + keep_ref[...] * (branch + norm_ref[5:6, :])
    out_ref[...] = out[: out_ref.shape[0]].astype(BF)


def rope_tables(coords):
    half_dim = HD // 2
    index_j = jnp.arange(half_dim // 2).astype(F32)
    frequency = jnp.repeat(jnp.exp(index_j * (-2.0 * math.log(10000.0) / half_dim)), 2)
    spots = jnp.arange(GRID_SIDE)
    angles = (spots.astype(F32) * 0.5)[:, None] * frequency
    lane_half = jnp.arange(LANES) // half_dim % 2
    tables = jnp.stack([jnp.cos(angles), jnp.sin(angles)])
    tables = jnp.tile(tables, (1, 1, LANES // half_dim))
    tables = jnp.concatenate([tables * (lane_half == half) for half in range(2)], axis=1)
    chosen = jnp.concatenate(
        [(coords[half][:, None] == spots).astype(F32) for half in range(2)], axis=1
    )
    both = jnp.dot(
        chosen,
        jnp.concatenate([tables[0], tables[1]], axis=1),
        precision=lax.Precision.HIGHEST,
    )
    return both[:, :LANES], both[:, LANES:]


def pad_to(value, axis, size):
    widths = [(0, 0)] * value.ndim
    widths[axis] = (0, size - value.shape[axis])
    return jnp.pad(value, widths)


def ceil_to(value, unit):
    return -(-value // unit) * unit


def on_device(
    n_dp,
    n_tp,
    tokens,
    cotangent,
    w_qkv,
    w_o,
    w_gu,
    w_down,
    norm_params,
    head_params,
    ffn_params,
    token_mask,
    empty_flag,
    coords,
):
    tp_index = lax.axis_index("tensor")
    own_rows, width = tokens.shape[1:]
    local = w_qkv.shape[2]
    units = w_gu.shape[2]
    heads = local // HD
    rows = ceil_to(own_rows, 16)
    seq = rows * n_tp
    lanes = ceil_to(units, LANES)
    step_rows, steps = seq, 1
    offsets = ring_offsets(n_tp)
    order = (jnp.array(offsets, jnp.int32) + tp_index) % n_tp
    place = {offset % n_tp: at for at, offset in enumerate(offsets)}
    own = whole((rows, width))

    normed = call(
        first_norm_body,
        (tokens[0], norm_params),
        [whole((own_rows, width)), whole(norm_params.shape)],
        [sds((rows, width), BF)],
        [own],
        (1,),
        us=1.2,
    )[0]
    normed_parts = ring_gather(normed, n_tp)

    ups = n_tp // 2
    arrivals = [[0]]
    for s in range(1, ups + 1):
        arrivals.append(sorted({place[-s % n_tp], place[s % n_tp]}))
    leaving = sorted({place[ups % n_tp], place[-1 % n_tp]})
    staying = [at for at in range(n_tp) if at not in leaving]
    leavings = [group for group in (leaving, staying) if group]

    slots = jnp.concatenate([token_mask, coords[0]], axis=0).reshape(3, n_tp, own_rows)
    slots = pad_to(slots, 2, rows)
    slots = jnp.stack(
        [lax.dynamic_index_in_dim(slots, order[at], 1, keepdims=False) for at in range(n_tp)], 1
    )
    mask = slots[0]
    bias = jnp.where(mask > 0, 0.0, -1e30).astype(F32)
    bias_row, bias_col = bias.reshape(1, seq), bias.reshape(seq, 1)
    keep = (mask[0].astype(F32) * (1.0 - empty_flag[0].astype(F32)))[:, None]
    cos_all, sin_all = rope_tables(slots[1:].reshape(2, seq))

    head_local = lax.dynamic_slice_in_dim(head_params, tp_index * local, local, 1)
    ffn_local = pad_to(
        lax.dynamic_slice_in_dim(ffn_params, tp_index * units, units, 1), 1, lanes
    )
    lane_at = jnp.arange(lanes)
    unit_row = ((lane_at < units) & (tp_index * units + lane_at < FF)).astype(F32)[None]

    tokens_own = pad_to(tokens[0], 0, rows)
    dy_own = pad_to(cotangent[0], 0, rows)
    d_low = (keep * dy_own.astype(F32)).astype(BF)

    w_order = dp_order(n_dp)
    full_qkv = put_back(w_order, dp_gather(w_qkv, n_dp), 1)
    filled = ()
    for turn, group in enumerate(arrivals):
        if turn > 1:
            normed_parts[group[0]] = after(normed_parts[group[0]], filled[0])
        filled = call(
            functools.partial(project_body, len(group)),
            (
                jnp.array(group, jnp.int32),
                *(normed_parts[at] for at in group),
                full_qkv,
                head_local,
                cos_all,
                sin_all,
            ),
            [own] * len(group)
            + [whole(full_qkv.shape), whole(head_local.shape)]
            + [pl.BlockSpec((rows, LANES), lambda s, place, *_: (place[s], 0))] * 2,
            [sds((n_tp, rows, local), BF)] * 3,
            [placed((rows, local))] * 3,
            (len(group),),
            scratch=[pltpu.VMEM((rows, width), BF)],
            prefetch=1,
            held=filled,
            us=2.0 * len(group),
        )
    query, key, value = (part.reshape(seq, local) for part in filled)
    d_low_late = after(d_low, normed_parts[-1], normed_parts[ups])
    d_low_first = [ring_up(d_low_late, n_tp), ring_down(d_low_late, n_tp)]
    strip = pl.BlockSpec((step_rows, local), lambda s, *_: (s, 0))
    mixed_heads, lse = call(
        attend_body,
        (order, query, key, value, bias_row),
        [strip, whole((seq, local)), whole((seq, local)), whole((1, seq))],
        [sds((n_tp, rows, local), BF), sds((steps, heads, step_rows), F32)],
        [whole((n_tp, rows, local)), lead((heads, step_rows))],
        (steps,),
        prefetch=1,
        us=10,
    )
    w_o_late = after(w_o, normed_parts[1])
    o_parts = call(
        lay_body,
        (order, *ring_gather(w_o_late, n_tp)),
        [whole(w_o.shape)] * n_tp,
        [sds((n_tp,) + w_o.shape[::-1], BF)],
        [whole((n_tp,) + w_o.shape[::-1])],
        (1,),
        prefetch=1,
        us=0.7,
    )[0]
    o_parts = jnp.concatenate([o_parts[at] for at in range(n_tp)], axis=1)
    full_o = put_back(w_order, dp_gather(o_parts, n_dp), 0)
    w_ffn = pad_to(jnp.concatenate([w_gu, w_down.T[None]], axis=0), 2, lanes)
    w_ffn = dp_gather(after(w_ffn, normed_parts[1]), n_dp)
    mixed_heads = after(mixed_heads, full_o, *d_low_first)
    mixed = lax.all_to_all(mixed_heads, "tensor", split_axis=0, concat_axis=0, tiled=True)

    inner_low, middle, normed_two = call(
        middle_body,
        (mixed, tokens_own, keep, full_o, norm_params, head_params),
        [
            whole(mixed.shape),
            own,
            whole((rows, 1)),
            whole(full_o.shape),
            whole(norm_params.shape),
            whole(head_params.shape),
        ],
        [sds((rows, width), BF), sds((rows, width), F32), sds((rows, width), BF)],
        [own] * 3,
        (1,),
        us=3,
    )
    two_parts = ring_gather(normed_two, n_tp)
    full_ffn = put_back(w_order, [after(part, normed_two) for part in w_ffn], 1)
    d_low_parts = gather_rest(d_low, d_low_first, n_tp, mixed)

    hidden_shape = (n_tp, rows, lanes)
    gu_block = pl.BlockSpec((2, width, lanes), lambda *_: (0, 0, 0))
    down_block = pl.BlockSpec((1, width, lanes), lambda *_: (2, 0, 0))
    d_ffn = [None] * n_tp
    near = [at for group in arrivals[:2] for at in group]
    for group in [near] + arrivals[2:]:
        outs = call(
            functools.partial(d_ffn_body, len(group)),
            (*(d_low_parts[at] for at in group), full_ffn),
            [own] * len(group) + [down_block],
            [sds((rows, lanes), F32)] * len(group),
            [whole((rows, lanes))] * len(group),
            (len(group),),
            scratch=[pltpu.VMEM((rows, width), BF)],
            us=1.4 * len(group),
        )
        for at, part in zip(group, outs):
            d_ffn[at] = part
    hidden_block = placed((rows, lanes))
    filled = ()
    for turn, group in enumerate(arrivals):
        if turn > 1:
            two_parts[group[0]] = after(two_parts[group[0]], filled[0])
        filled = call(
            functools.partial(ffn_body, len(group)),
            (
                jnp.array(group, jnp.int32),
                order,
                *(two_parts[at] for at in group),
                *(d_ffn[at] for at in group),
                full_ffn,
                ffn_local,
                unit_row,
            ),
            [own] * len(group)
            + [whole((rows, lanes))] * len(group)
            + [gu_block, whole(ffn_local.shape), whole(unit_row.shape)],
            [sds(hidden_shape, F32)] * 2 + [sds((n_tp, 4, rows), F32)],
            [hidden_block] * 2 + [ordered((4, rows))],
            (len(group),),
            scratch=[pltpu.VMEM((rows, width), BF), pltpu.VMEM((rows, lanes), F32)],
            prefetch=2,
            held=filled,
            us=1.2 + 2.2 * len(group),
        )
    gate, up, stats = filled
    stats = jnp.swapaxes(sum_shifts(stats, n_tp), 1, 2)
    filled, ffn_sums, d_two_parts = (), 0.0, [None] * n_tp
    for group in leavings:
        outs = call(
            functools.partial(ffn_back_body, len(group)),
            (
                jnp.array(group, jnp.int32),
                order,
                gate,
                up,
                *(d_ffn[at] for at in group),
                stats,
                full_ffn,
                ffn_local,
                unit_row,
            ),
            [hidden_block] * 2
            + [whole((rows, lanes))] * len(group)
            + [
                ordered((rows, 4)),
                gu_block,
                whole(ffn_local.shape),
                whole(unit_row.shape),
            ],
            [sds(hidden_shape, BF)] * 3
            + [sds((4, lanes), F32)]
            + [sds((rows, width), BF)] * len(group),
            [hidden_block] * 3 + [whole((4, lanes))] + [own] * len(group),
            (len(group),),
            scratch=[pltpu.VMEM((rows, lanes), F32)],
            prefetch=2,
            held=filled,
            us=3.7 * len(group),
        )
        filled = outs[:3]
        ffn_sums = ffn_sums + outs[3]
        for at, piece in zip(group, outs[4:]):
            d_two_parts[at] = piece
    ffn_low, d_gate, d_up = filled
    d_two_first = scatter_first(d_two_parts, n_tp)
    d_two_first = [after(d_two_first[0], *d_two_first[1:])] + d_two_first[1:]
    d_two_terms = scatter_rest(d_two_parts, d_two_first, n_tp)
    branch_parts = call(
        functools.partial(down_body, n_tp),
        (ffn_low, full_ffn),
        [lead((rows, lanes)), down_block],
        [sds((rows, width), BF)] * n_tp,
        [own] * n_tp,
        (n_tp,),
        us=2.8,
    )

    d_two_terms[0] = after(d_two_terms[0], *branch_parts)

    parity = (lax.axis_index("dp") % 2).astype(jnp.int32)[None]
    block = width // n_dp
    hidden_rows = [part.reshape(seq, lanes) for part in (d_gate, d_up, ffn_low)]
    grad_ffn = product([two_parts, d_low_parts], [hidden_rows[:2], hidden_rows[2:]], parity, block)
    grad_ffn = pair_sum(grad_ffn, n_dp)


    n_terms = len(d_two_terms)
    d_middle, d_branch, d_mixed_rows, mid_sums = call(
        functools.partial(middle_back_body, n_terms),
        (*d_two_terms, middle, dy_own, d_low, keep, mixed, full_o, norm_params, head_params),
        [own] * n_terms
        + [own] * 3
        + [
            whole((rows, 1)),
            whole(mixed.shape),
            whole(full_o.shape),
            whole(norm_params.shape),
            whole(head_params.shape),
        ],
        [
            sds((rows, width), F32),
            sds((rows, width), BF),
            sds((n_tp, rows, local), BF),
            sds((8, width), F32),
        ],
        [own, own, whole((n_tp, rows, local)), whole((8, width))],
        (1,),
        us=3.6,
    )
    d_mixed = lax.all_to_all(d_mixed_rows, "tensor", split_axis=0, concat_axis=0, tiled=True)
    d_mixed = after(d_mixed, grad_ffn)
    grad_ffn = dp_scatter(grad_ffn, n_dp)
    branch_parts = [after(part, d_mixed) for part in branch_parts]
    branch_first = scatter_first(branch_parts, n_tp)

    table = pl.BlockSpec((step_rows, LANES), lambda s, *_: (s, 0))
    all_rows = whole((seq, local))
    d_query, d_key, d_value, head_sums = call(
        attend_back_body,
        (
            order,
            query,
            d_mixed,
            lse,
            key,
            value,
            bias_col,
            cos_all,
            sin_all,
            cos_all,
            sin_all,
        ),
        [
            strip,
            whole(d_mixed.shape),
            lead((heads, step_rows)),
            all_rows,
            all_rows,
            whole((seq, 1)),
            table,
            table,
            whole((seq, LANES)),
            whole((seq, LANES)),
        ],
        [sds((seq, local), BF)] * 3 + [sds((8, local), F32)],
        [strip, all_rows, all_rows, whole((8, local))],
        (steps,),
        scratch=[pltpu.VMEM((seq, local), F32)] * 2,
        prefetch=1,
        us=24,
    )
    d_query = after(d_query, *branch_first)
    chunk = pl.BlockSpec((rows, local), lambda s, place, *_: (place[s], 0))
    d_one_parts = [None] * n_tp
    for group in leavings:
        outs = call(
            functools.partial(spread_back_body, len(group)),
            (jnp.array(group, jnp.int32), d_query, d_key, d_value, full_qkv),
            [chunk] * 3 + [whole(full_qkv.shape)],
            [sds((rows, width), BF)] * len(group),
            [own] * len(group),
            (len(group),),
            prefetch=1,
            us=1.0 * len(group),
        )
        for at, piece in zip(group, outs):
            d_one_parts[at] = piece
    d_proj = [after(part, *[d_one_parts[at] for at in leaving]) for part in (d_query, d_key, d_value)]
    *grad_late, along_normed = product(
        [normed_parts, [d_branch]], [d_proj, [inner_low]], parity, block, full_qkv
    )
    along_normed = along_normed.reshape(-1)
    shift_one = sum(
        jnp.sum(full_qkv[at].astype(F32) * head_sums[at : at + 1], axis=1) for at in range(3)
    )
    grad_late = pair_sum(grad_late, n_dp)

    d_one_first = scatter_first(d_one_parts, n_tp)
    arrived = [after(d_one_first[0], grad_late, grad_ffn)] + d_one_first[1:]
    sent = []
    d_one_terms = scatter_rest(d_one_parts, arrived, n_tp, sent)

    small = [along_normed, shift_one, mid_sums[:6].reshape(-1)]
    small += [head_sums[0], head_sums[2], ffn_sums[:, :units].reshape(-1)]
    small = jnp.concatenate(small)
    small_len = small.shape[0]
    small = pad_to(small, 0, ceil_to(small_len, 8 * LANES)).reshape(-1, LANES)
    small = sum_over(after(small, grad_ffn), "dp", n_dp)
    small_sum = small
    grad_late = dp_scatter(after(grad_late, small), n_dp)
    late_parts = grad_late
    small = after(small, *sent)
    small = [part.reshape(-1) for part in gather_small(small, n_tp)]
    head_at = 8 * width
    ffn_at = head_at + 2 * local
    norm_sums = sum_alike([part[:head_at] for part in small]).reshape(8, width)
    head_bias = jnp.zeros((2, width), F32)
    ffn_total = jnp.zeros((4, n_tp * units), F32)
    for s, part in enumerate(small):
        owner = (tp_index - s) % n_tp
        head_bias = lax.dynamic_update_slice(
            head_bias, part[head_at:ffn_at].reshape(2, local), (0, owner * local)
        )
        ffn_total = lax.dynamic_update_slice(
            ffn_total, part[ffn_at:small_len].reshape(4, units), (0, owner * units)
        )
    gain_one = (norm_sums[0:1] - norm_params[1:2] * norm_sums[1:2]) / norm_params[0:1]
    norm_total = jnp.concatenate([gain_one, norm_sums[1:6]], axis=0)
    head_total = jnp.concatenate([head_bias, norm_sums[6:8]], axis=0)

    grad_early = sum_parts(grad_ffn)
    grad_late = sum_parts(grad_late)
    grad_o = grad_late[:, 3 * local :].astype(BF).reshape(-1, n_tp, local).swapaxes(0, 1)
    grad_o = swap_sum(grad_o, n_tp).T
    grad_gu = jnp.stack([grad_early[:, :units], grad_early[:, lanes : lanes + units]])
    grad_down = grad_early[:, 2 * lanes : 2 * lanes + units].T
    grad_qkv = grad_late[:, : 3 * local].reshape(-1, 3, local).swapaxes(0, 1)

    branch_first = [after(branch_first[0], small_sum)] + branch_first[1:]
    branch_terms = scatter_rest(branch_parts, branch_first, n_tp)
    branch_terms[1] = after(branch_terms[1], late_parts)
    layer_out = call(
        functools.partial(layer_out_body, n_terms),
        (*branch_terms, middle, keep, norm_params),
        [own] * n_terms + [own, whole((rows, 1)), whole(norm_params.shape)],
        [sds((own_rows, width), BF)],
        [whole((own_rows, width))],
        (1,),
        us=2,
    )[0]
    d_one_terms[0] = after(d_one_terms[0], grad_late, norm_total, ffn_total)
    d_tokens = call(
        functools.partial(first_back_body, n_terms),
        (*d_one_terms, tokens[0], d_middle, norm_params),
        [own] * n_terms + [whole((own_rows, width)), own, whole(norm_params.shape)],
        [sds((own_rows, width), F32)],
        [whole((own_rows, width))],
        (1,),
        us=1.5,
    )[0]

    return (
        layer_out[None],
        d_tokens[None],
        grad_qkv,
        grad_o,
        grad_gu,
        grad_down,
        norm_total,
        head_total,
        ffn_total,
    )


def solution(mesh):
    placed = (
        P("dp", "tensor", None),
        P("dp", "tensor", None),
        P(None, "dp", "tensor"),
        P("tensor", "dp"),
        P(None, "dp", "tensor"),
        P("tensor", "dp"),
        P(),
        P(),
        P(),
        P("dp", None),
        P("dp"),
        P("dp", None, None),
    )
    return jax.shard_map(
        functools.partial(on_device, mesh.shape["dp"], mesh.shape["tensor"]),
        mesh=mesh,
        in_specs=placed,
        out_specs=(
            P("dp", "tensor", None),
            P("dp", "tensor", None),
            P(None, "dp", "tensor"),
            P("tensor", "dp"),
            P(None, "dp", "tensor"),
            P("tensor", "dp"),
            P(),
            P(),
            P(),
        ),
        check_vma=False,
    )
```

profile of v0, /device:TPU:0, one launch (start us, length us, event | category | flops | bytes accessed | tf_op | source)
XLA Modules:
  0.0 368.4 jit_solution(4900404070164800501)
XLA Ops:
  25.9 8.5 %collective-permute-start.8 = (bf16[256,128]{1,0:T(8,128)(2,1)S(1)}, bf16[256,128]{1,0:T(8,128)(2,1)S(1)}, u32[]{:S(2)}, u32[]{:S(2)}) collective-permute-start(bf16[256,128]{1,0:T(8,128)(2,1)S(1)} %copy-done.43), channel_id=1, source_target_pairs={{0,3},{1,0},{2,1},{3,2},{4,7},{5,4},{6,5},{7,6},{8,11},{9,8},{10,9... | collective-permute-start | bytes 196616 | tf_op jit(solution)/shard_map/ppermute | solution.py:30
  37.8 4.9 %collective-permute-done.7.refs_2_ = bf16[256,128]{1,0:T(8,128)(2,1)S(1)} collective-permute-done((bf16[256,128]{1,0:T(8,128)(2,1)S(1)}, bf16[256,128]{1,0:T(8,128)(2,1)S(1)}, u32[]{:S(2)}, u32[]{:S(2)}) %collective-permute-start.7) | collective-permute-done | bytes 65568 | tf_op jit(solution)/shard_map/ppermute | solution.py:26
  47.0 3.8 %collective-permute-done.9 = bf16[1,128,1024]{2,1,0:T(8,128)(2,1)} collective-permute-done((bf16[1,128,1024]{2,1,0:T(8,128)(2,1)}, bf16[1,128,1024]{2,1,0:T(8,128)(2,1)}, u32[]{:S(2)}, u32[]{:S(2)}) %collective-permute-start.9) | collective-permute-done | bytes 262176 | tf_op jit(solution)/shard_map/ppermute | solution.py:141
  63.1 4.0 %collective-permute-start.13 = (bf16[272,1024]{1,0:T(8,128)(2,1)S(1)}, bf16[272,1024]{1,0:T(8,128)(2,1)S(1)}, u32[]{:S(2)}, u32[]{:S(2)}) collective-permute-start(bf16[272,1024]{1,0:T(8,128)(2,1)S(1)} %multiply_convert_fusion.refs_0_.refs_5_.refs_4_), channel_id=1, source_target_pairs={{0,3},{1,0},{2,1},{3,2},{4,7},{5,4},{6,5},{7,6},{8,11},{9,8},{10,9... | collective-permute-start | bytes 1671176 | tf_op jit(solution)/shard_map/ppermute | solution.py:30
  69.5 10.7 %shard_map.300 = (bf16[4,272,256]{2,1,0:T(8,128)(2,1)}, f32[1,4,1088]{2,1,0:T(4,128)S(1)}) custom-call(s32[4]{0:T(128)S(1)} %and_select_fusion.2.order_ref, bf16[1088,256]{1,0:T(8,128)(2,1)S(1)} %bitcast.92, bf16[1088,256]{1,0:T(8,128)(2,1)S(1)} %bitcast.94, bf16[1088,256]{1,0:T(8,128)(2,1)S(1)} %bitcast.96, f32[1,1088]{1,0:T(1,128)S(1)} %select_n.161.bias_ref), custom_call_target="tpu_custom_call" | custom-call | flops 40000000000 | bytes 1 | tf_op jit(solution)/shard_map/pallas_call | solution.py:207
  82.5 3.7 %collective-permute-done.13.refs_2_.refs_7_ = bf16[272,1024]{1,0:T(8,128)(2,1)S(1)} collective-permute-done((bf16[272,1024]{1,0:T(8,128)(2,1)S(1)}, bf16[272,1024]{1,0:T(8,128)(2,1)S(1)}, u32[]{:S(2)}, u32[]{:S(2)}) %collective-permute-start.13) | collective-permute-done | bytes 557088 | tf_op jit(solution)/shard_map/ppermute | solution.py:30
  87.1 4.5 %all-to-all-start = ((bf16[4,272,256]{2,1,0:T(8,128)(2,1)}), bf16[4,272,256]{2,1,0:T(8,128)(2,1)S(1)}, u32[]{:S(2)}, u32[]{:S(2)}) async-start(bf16[4,272,256]{2,1,0:T(8,128)(2,1)} %get-tuple-element.108), calls=%async_computation | async-start | bytes 1114112 | tf_op jit(solution)/shard_map/all_to_all | solution.py:821
  96.2 9.1 %all-to-all-done.mixed_ref.refs_7_ = bf16[4,272,256]{2,1,0:T(8,128)(2,1)S(1)} async-done(((bf16[4,272,256]{2,1,0:T(8,128)(2,1)}), bf16[4,272,256]{2,1,0:T(8,128)(2,1)S(1)}, u32[]{:S(2)}, u32[]{:S(2)}) %all-to-all-start) | async-done | bytes 557088 | tf_op jit(solution)/shard_map/all_to_all | solution.py:821
  113.8 3.8 %collective-permute-start.16 = (bf16[272,1024]{1,0:T(8,128)(2,1)}, bf16[272,1024]{1,0:T(8,128)(2,1)S(1)}, u32[]{:S(2)}, u32[]{:S(2)}) collective-permute-start(bf16[272,1024]{1,0:T(8,128)(2,1)} %get-tuple-element.109.refs_0_), channel_id=1, source_target_pairs={{0,3},{1,0},{2,1},{3,2},{4,7},{5,4},{6,5},{7,6},{8,11},{9,8},{10,9... | collective-permute-start | bytes 1671176 | tf_op jit(solution)/shard_map/ppermute | solution.py:30
  117.7 13.7 %collective-permute-done.14.refs_0_.refs_1_ = bf16[272,1024]{1,0:T(8,128)(2,1)} collective-permute-done((bf16[272,1024]{1,0:T(8,128)(2,1)}, bf16[272,1024]{1,0:T(8,128)(2,1)}, u32[]{:S(2)}, u32[]{:S(2)}) %collective-permute-start.14) | collective-permute-done | bytes 557088 | tf_op jit(solution)/shard_map/ppermute | solution.py:26
  131.3 6.1 %collective-permute-start.15 = (bf16[272,1024]{1,0:T(8,128)(2,1)}, bf16[272,1024]{1,0:T(8,128)(2,1)S(1)}, u32[]{:S(2)}, u32[]{:S(2)}) collective-permute-start(bf16[272,1024]{1,0:T(8,128)(2,1)} %collective-permute-done.14.refs_0_.refs_1_), channel_id=1, source_target_pairs={{0,1},{1,2},{2,3},{3,0},{4,5},{5,6},{6,7},{7,4},{8,9},{9,10},{10,1... | collective-permute-start | bytes 1671176 | tf_op jit(solution)/shard_map/ppermute | solution.py:26
  137.4 4.4 %shard_map.304.refs_3_.refs_2_.refs_4_.refs_1_.refs_5_.w_ref = bf16[3,1024,768]{2,1,0:T(8,128)(2,1)S(1)} custom-call(s32[8]{0:T(128)S(1)} %broadcast_xor_fusion.refs_0_, bf16[4,3,128,768]{3,2,1,0:T(8,128)(2,1)S(1)} %pad_maximum_fusion.refs_1_, bf16[4,3,128,768]{3,2,1,0:T(8,128)(2,1)} %collective-permute-done.19.refs_2_), custom_call_target="tpu_custom_call" | custom-call | flops 17999998976 | bytes 1 | tf_op jit(solution)/shard_map/pallas_call | solution.py:207
  144.0 5.0 %shard_map.306 = (f32[4,272,768]{2,1,0:T(8,128)S(1)}, f32[4,272,768]{2,1,0:T(8,128)S(1)}, f32[4,4,272]{2,1,0:T(4,128)S(1)}) custom-call(s32[1]{0:T(128)} %constant.167.clone.place_ref, s32[4]{0:T(128)S(1)} %and_select_fusion.2.order_ref, bf16[272,1024]{1,0:T(8,128)(2,1)} %get-tuple-element.109.refs_0_, f32[272,768]{1,0:T(8,128)S(1)} %get-tuple-element.115.refs_1_.refs_2_, ...), custom_call_target="tpu_custom_call" | custom-call | flops 13600000000 | bytes 1 | tf_op jit(solution)/shard_map/pallas_call | solution.py:207
  149.1 5.4 %shard_map.307 = (f32[4,272,768]{2,1,0:T(8,128)S(1)}, f32[4,272,768]{2,1,0:T(8,128)S(1)}, f32[4,4,272]{2,1,0:T(4,128)S(1)}) custom-call(s32[2]{0:T(128)S(1)} %copy-done.54, s32[4]{0:T(128)S(1)} %and_select_fusion.2.order_ref, bf16[272,1024]{1,0:T(8,128)(2,1)} %collective-permute-done.14.refs_0_.refs_1_, ...), custom_call_target="tpu_custom_call", output_to_operand_aliasing={{0}: (9, {}), {1}: (10, {}), {2}: (11, {})} | custom-call | flops 22400000000 | bytes 1 | tf_op jit(solution)/shard_map/pallas_call | solution.py:207
  154.6 10.1 %collective-permute-done.15.refs_0_.refs_2_ = bf16[272,1024]{1,0:T(8,128)(2,1)S(1)} collective-permute-done((bf16[272,1024]{1,0:T(8,128)(2,1)}, bf16[272,1024]{1,0:T(8,128)(2,1)S(1)}, u32[]{:S(2)}, u32[]{:S(2)}) %collective-permute-start.15) | collective-permute-done | bytes 557088 | tf_op jit(solution)/shard_map/ppermute | solution.py:26
  165.7 3.7 %shard_map.309 = (f32[4,272,768]{2,1,0:T(8,128)S(1)}, f32[4,272,768]{2,1,0:T(8,128)S(1)}, f32[4,4,272]{2,1,0:T(4,128)S(1)}) custom-call(s32[1]{0:T(128)} %constant.169.clone.place_ref, s32[4]{0:T(128)S(1)} %and_select_fusion.2.order_ref, ...), custom_call_target="tpu_custom_call", output_to_operand_aliasing={{0}: (7, {}), {1}: (8, {}), {2}: (9, {})} | custom-call | flops 13600000000 | bytes 1 | tf_op jit(solution)/shard_map/pallas_call | solution.py:207
  183.5 7.5 %shard_map.310 = (bf16[4,272,768]{2,1,0:T(8,128)(2,1)S(1)}, bf16[4,272,768]{2,1,0:T(8,128)(2,1)S(1)}, bf16[4,272,768]{2,1,0:T(8,128)(2,1)S(1)}, f32[4,768]{1,0:T...) custom-call(s32[2]{0:T(128)S(1)} %copy-done.52, s32[4]{0:T(128)S(1)} %and_select_fusion.2.order_ref, ...), custom_call_target="tpu_custom_call" | custom-call | flops 29600000000 | bytes 1 | tf_op jit(solution)/shard_map/pallas_call | solution.py:207
  191.5 3.8 %collective-permute-start.25 = (bf16[272,1024]{1,0:T(8,128)(2,1)S(1)}, bf16[272,1024]{1,0:T(8,128)(2,1)S(1)}, u32[]{:S(2)}, u32[]{:S(2)}) collective-permute-start(bf16[272,1024]{1,0:T(8,128)(2,1)S(1)} %get-tuple-element.138), channel_id=1, source_target_pairs={{0,3},{1,0},{2,1},{3,2},{4,7},{5,4},{6,5},{7,6},{8,11},{9,8},{10,9... | collective-permute-start | bytes 1671176 | tf_op jit(solution)/shard_map/ppermute | solution.py:30
  195.3 7.7 %shard_map.311 = (bf16[4,272,768]{2,1,0:T(8,128)(2,1)S(1)}, bf16[4,272,768]{2,1,0:T(8,128)(2,1)S(1)}, bf16[4,272,768]{2,1,0:T(8,128)(2,1)S(1)}, f32[4,768]{1,0:T...) custom-call(s32[2]{0:T(128)S(1)} %iota_multiply_fusion.place_ref, ...), custom_call_target="tpu_custom_call", output_to_operand_aliasing={{0}: (10, {}), {1}: (11, {}), {2}: (12, {})} | custom-call | flops 29600000000 | bytes 1 | tf_op jit(solution)/shard_map/pallas_call | solution.py:207
  203.1 9.4 %shard_map.314 = (bf16[4,128,2304]{2,1,0:T(8,128)(2,1)}, bf16[4,128,2304]{2,1,0:T(8,128)(2,1)}) custom-call(s32[1]{0:T(128)} %bitcast.23.parity_ref, bf16[272,1024]{1,0:T(8,128)(2,1)} %get-tuple-element.109.refs_0_, bf16[272,1024]{1,0:T(8,128)(2,1)} %collective-permute-done.14.refs_0_.refs_1_, bf16[272,1024]{1,0:T(8,128)(2,1)S(1)} %copy-done.35, ...), custom_call_target="tpu_custom_call" | custom-call | flops 36864000000 | bytes 1 | tf_op jit(solution)/shard_map/pallas_call | solution.py:207
  225.1 5.8 %collective-permute-done.26.refs_1_ = bf16[272,1024]{1,0:T(8,128)(2,1)} collective-permute-done((bf16[272,1024]{1,0:T(8,128)(2,1)}, bf16[272,1024]{1,0:T(8,128)(2,1)}, u32[]{:S(2)}, u32[]{:S(2)}) %collective-permute-start.26) | collective-permute-done | bytes 557088 | tf_op jit(solution)/shard_map/ppermute | solution.py:26
  235.8 4.2 %shard_map.313 = (f32[272,1024]{1,0:T(8,128)S(1)}, bf16[272,1024]{1,0:T(8,128)(2,1)S(1)}, bf16[4,272,256]{2,1,0:T(8,128)(2,1)}, f32[8,1024]{1,0:T(8,128)S(1)}) custom-call(bf16[272,1024]{1,0:T(8,128)(2,1)S(1)} %copy-done.82, bf16[272,1024]{1,0:T(8,128)(2,1)} %collective-permute-done.26.refs_1_, bf16[272,1024]{1,0:T(8,128)(2,1)S(1)} %copy-done.42, ...), custom_call_target="tpu_custom_call" | custom-call | flops 14400000000 | bytes 1 | tf_op jit(solution)/shard_map/pallas_call | solution.py:207
  245.3 4.3 %add_convert_fusion = bf16[4,128,2304]{2,1,0:T(8,128)(2,1)} fusion(bf16[4,128,2304]{2,1,0:T(8,128)(2,1)} %collective-permute-done.27, bf16[4,128,2304]{2,1,0:T(8,128)(2,1)} %get-tuple-element.145), kind=kLoop, calls=%fused_computation.1 | loop fusion | flops 4718592 | bytes 7077888 | tf_op jit(solution)/shard_map/convert_element_type | solution.py:96
  249.7 8.9 %all-to-all-done.1.dmix_ref = bf16[4,272,256]{2,1,0:T(8,128)(2,1)S(1)} async-done(((bf16[4,272,256]{2,1,0:T(8,128)(2,1)}), bf16[4,272,256]{2,1,0:T(8,128)(2,1)S(1)}, u32[]{:S(2)}, u32[]{:S(2)}) %all-to-all-start.1) | async-done | bytes 557088 | tf_op jit(solution)/shard_map/all_to_all | solution.py:973
  258.6 4.5 %all-to-all-start.2 = ((bf16[4,128,2304]{2,1,0:T(8,128)(2,1)}), bf16[4,128,2304]{2,1,0:T(8,128)(2,1)}, u32[]{:S(2)}, u32[]{:S(2)}) async-start(bf16[4,128,2304]{2,1,0:T(8,128)(2,1)} %add_convert_fusion), calls=%async_computation.2 | async-start | bytes 4718592 | tf_op jit(solution)/shard_map/all_to_all | solution.py:169
  268.5 18.8 %shard_map.315 = (bf16[1088,256]{1,0:T(8,128)(2,1)S(1)}, bf16[1088,256]{1,0:T(8,128)(2,1)S(1)}, bf16[1088,256]{1,0:T(8,128)(2,1)S(1)}, f32[8,256]{1,0:T(8,128)S(1)}) custom-call(s32[4]{0:T(128)S(1)} %and_select_fusion.2.order_ref, bf16[1088,256]{1,0:T(8,128)(2,1)S(1)} %bitcast.93, bf16[4,272,256]{2,1,0:T(8,128)(2,1)S(1)} %all-to-all-done.1.dmix_ref, ...), custom_call_target="tpu_custom_call" | custom-call | flops 96000000000 | bytes 1 | tf_op jit(solution)/shard_map/pallas_call | solution.py:207
  296.3 6.0 %shard_map.317 = (bf16[4,128,1792]{2,1,0:T(8,128)(2,1)S(1)}, bf16[4,128,1792]{2,1,0:T(8,128)(2,1)}, f32[4,1,256]{2,1,0:T(1,128)S(1)}) custom-call(s32[1]{0:T(128)} %bitcast.23.parity_ref, bf16[272,1024]{1,0:T(8,128)(2,1)} %shard_map.295.refs_0_, bf16[272,1024]{1,0:T(8,128)(2,1)S(1)} %copy-done.21, bf16[272,1024]{1,0:T(8,128)(2,1)S(1)} %copy-done.23, ...), custom_call_target="tpu_custom_call" | custom-call | flops 28672000000 | bytes 1 | tf_op jit(solution)/shard_map/pallas_call | solution.py:207
  306.0 4.2 %all-to-all-start.3 = ((f32[8,96,128]{2,1,0:T(8,128)}), f32[8,96,128]{2,1,0:T(8,128)S(1)}, u32[]{:S(2)}, u32[]{:S(2)}) async-start(f32[8,96,128]{2,1,0:T(8,128)} %broadcast_in_dim.61), calls=%async_computation.3 | async-start | bytes 786432 | tf_op jit(solution)/shard_map/all_to_all | solution.py:180
  323.9 4.4 %all-to-all-start.4 = ((bf16[4,128,1792]{2,1,0:T(8,128)(2,1)}), bf16[4,128,1792]{2,1,0:T(8,128)(2,1)}, u32[]{:S(2)}, u32[]{:S(2)}) async-start(bf16[4,128,1792]{2,1,0:T(8,128)(2,1)} %add_convert_fusion.1), calls=%async_computation.4 | async-start | bytes 3670016 | tf_op jit(solution)/shard_map/all_to_all | solution.py:169
  331.0 3.8 %collective-permute-start.33 = (f32[96,128]{1,0:T(8,128)S(1)}, f32[96,128]{1,0:T(8,128)S(1)}, u32[]{:S(2)}, u32[]{:S(2)}) collective-permute-start(f32[96,128]{1,0:T(8,128)S(1)} %reduce_sum.57), channel_id=1, source_target_pairs={{0,2},{1,3},{2,0},{3,1},{4,6},{5,7},{6,4},{7,5},{8,10},{9,11},{10,... | collective-permute-start | bytes 147464 | tf_op jit(solution)/shard_map/ppermute | solution.py:70
  343.6 7.3 %all-to-all-done.4 = bf16[4,128,1792]{2,1,0:T(8,128)(2,1)} async-done(((bf16[4,128,1792]{2,1,0:T(8,128)(2,1)}), bf16[4,128,1792]{2,1,0:T(8,128)(2,1)}, u32[]{:S(2)}, u32[]{:S(2)}) %all-to-all-start.4) | async-done | bytes 1835040 | tf_op jit(solution)/shard_map/all_to_all | solution.py:169
  355.2 3.9 %collective-permute-start.39 = (bf16[128,256]{0,1:T(8,128)(2,1)S(1)}, bf16[128,256]{0,1:T(8,128)(2,1)S(1)}, u32[]{:S(2)}, u32[]{:S(2)}) collective-permute-start(bf16[128,256]{0,1:T(8,128)(2,1)S(1)} %bitcast.109), channel_id=1, source_target_pairs={{0,2},{1,3},{2,0},{3,1},{4,6},{5,7},{6,4},{7,5},{8,10},{9,11},{10,... | collective-permute-start | bytes 196616 | tf_op jit(solution)/shard_map/ppermute | solution.py:90
  (417 shorter events, 151.3 us)
Async XLA Ops:
  3.7 22.1 %collective-permute-start = (bf16[272,1024]{1,0:T(8,128)(2,1)}, bf16[272,1024]{1,0:T(8,128)(2,1)S(1)}, u32[]{:S(2)}, u32[]{:S(2)}) collective-permute-start(bf16[272,1024]{1,0:T(8,128)(2,1)} %shard_map.295.refs_0_), channel_id=1, source_target_pairs={{0,1},{1,2},{2,3},{3,0},{4,5},{5,6},{6,7},{7,4},{8,9},{9,10},{10,1... | collective-permute-start | bytes 1671176 | tf_op jit(solution)/shard_map/ppermute | solution.py:26
  6.7 53.1 %collective-permute-start.2 = (bf16[272,1024]{1,0:T(8,128)(2,1)}, bf16[272,1024]{1,0:T(8,128)(2,1)}, u32[]{:S(2)}, u32[]{:S(2)}) collective-permute-start(bf16[272,1024]{1,0:T(8,128)(2,1)} %shard_map.295.refs_0_), channel_id=1, source_target_pairs={{0,3},{1,0},{2,1},{3,2},{4,7},{5,4},{6,5},{7,6},{8,11},{9,8},{10,9... | collective-permute-start | bytes 1671176 | tf_op jit(solution)/shard_map/ppermute | solution.py:30
  8.7 13.8 %collective-permute-start.3 = (bf16[1,3,128,256]{3,2,1,0:T(8,128)(2,1)S(1)}, bf16[1,3,128,256]{3,2,1,0:T(8,128)(2,1)S(1)}, u32[]{:S(2)}, u32[]{:S(2)}) collective-permute-start(bf16[1,3,128,256]{3,2,1,0:T(8,128)(2,1)S(1)} %bitcast.104), channel_id=1, source_target_pairs={{0,8},{4,12},{8,0},{12,4},{16,24},{20,28},{24,16},{28,20},{1,9},{5... | collective-permute-start | bytes 589832 | tf_op jit(solution)/shard_map/ppermute | solution.py:141
  22.6 14.0 %collective-permute-start.4 = (bf16[2,3,128,256]{3,2,1,0:T(8,128)(2,1)S(1)}, bf16[2,3,128,256]{3,2,1,0:T(8,128)(2,1)}, u32[]{:S(2)}, u32[]{:S(2)}) collective-permute-start(bf16[2,3,128,256]{3,2,1,0:T(8,128)(2,1)S(1)} %pad_maximum_fusion.6), channel_id=1, source_target_pairs={{0,16},{4,20},{8,24},{12,28},{16,0},{20,4},{24,8},{28,12},{1,17},{... | collective-permute-start | bytes 1179656 | tf_op jit(solution)/shard_map/ppermute | solution.py:141
  34.4 19.1 %collective-permute-start.17 = (bf16[1,3,128,768]{3,2,1,0:T(8,128)(2,1)}, bf16[1,3,128,768]{3,2,1,0:T(8,128)(2,1)}, u32[]{:S(2)}, u32[]{:S(2)}) collective-permute-start(bf16[1,3,128,768]{3,2,1,0:T(8,128)(2,1)} %bitcast.21), channel_id=1, source_target_pairs={{0,8},{4,12},{8,0},{12,4},{16,24},{20,28},{24,16},{28,20},{1,9},{5... | collective-permute-start | bytes 1769480 | tf_op jit(solution)/shard_map/ppermute | solution.py:141
  37.7 18.7 %collective-permute-start.5 = (bf16[4,3,128,256]{3,2,1,0:T(8,128)(2,1)S(1)}, bf16[4,3,128,256]{3,2,1,0:T(8,128)(2,1)S(1)}, u32[]{:S(2)}, u32[]{:S(2)}) collective-permute-start(bf16[4,3,128,256]{3,2,1,0:T(8,128)(2,1)S(1)} %pad_maximum_fusion.3.refs_1_), channel_id=1, source_target_pairs={{0,4},{4,0},{8,12},{12,8},{16,20},{20,16},{24,28},{28,24},{1,5},{5... | collective-permute-start | bytes 2359304 | tf_op jit(solution)/shard_map/ppermute | solution.py:141
  47.0 16.1 %collective-permute-start.1 = (bf16[272,1024]{1,0:T(8,128)(2,1)}, bf16[272,1024]{1,0:T(8,128)(2,1)S(1)}, u32[]{:S(2)}, u32[]{:S(2)}) collective-permute-start(bf16[272,1024]{1,0:T(8,128)(2,1)} %copy-done.19), channel_id=1, source_target_pairs={{0,1},{1,2},{2,3},{3,0},{4,5},{5,6},{6,7},{7,4},{8,9},{9,10},{10,1... | collective-permute-start | bytes 1671176 | tf_op jit(solution)/shard_map/ppermute | solution.py:26
  51.9 16.0 %collective-permute-start.10 = (bf16[2,128,1024]{2,1,0:T(8,128)(2,1)S(1)}, bf16[2,128,1024]{2,1,0:T(8,128)(2,1)S(1)}, u32[]{:S(2)}, u32[]{:S(2)}) collective-permute-start(bf16[2,128,1024]{2,1,0:T(8,128)(2,1)S(1)} %pad_maximum_fusion.5), channel_id=1, source_target_pairs={{0,16},{4,20},{8,24},{12,28},{16,0},{20,4},{24,8},{28,12},{1,17},{... | collective-permute-start | bytes 1572872 | tf_op jit(solution)/shard_map/ppermute | solution.py:141
  55.9 35.7 %collective-permute-start.18 = (bf16[2,3,128,768]{3,2,1,0:T(8,128)(2,1)}, bf16[2,3,128,768]{3,2,1,0:T(8,128)(2,1)}, u32[]{:S(2)}, u32[]{:S(2)}) collective-permute-start(bf16[2,3,128,768]{3,2,1,0:T(8,128)(2,1)} %pad_maximum_fusion.1), channel_id=1, source_target_pairs={{0,16},{4,20},{8,24},{12,28},{16,0},{20,4},{24,8},{28,12},{1,17},{... | collective-permute-start | bytes 3538952 | tf_op jit(solution)/shard_map/ppermute | solution.py:141
  63.1 19.5 %collective-permute-start.12 = (bf16[272,1024]{1,0:T(8,128)(2,1)S(1)}, bf16[272,1024]{1,0:T(8,128)(2,1)S(1)}, u32[]{:S(2)}, u32[]{:S(2)}) collective-permute-start(bf16[272,1024]{1,0:T(8,128)(2,1)S(1)} %multiply_convert_fusion.refs_0_.refs_5_.refs_4_), channel_id=1, source_target_pairs={{0,1},{1,2},{2,3},{3,0},{4,5},{5,6},{6,7},{7,4},{8,9},{9,10},{10,1... | collective-permute-start | bytes 1671176 | tf_op jit(solution)/shard_map/ppermute | solution.py:26
  63.1 23.1 %collective-permute-start.13 = (bf16[272,1024]{1,0:T(8,128)(2,1)S(1)}, bf16[272,1024]{1,0:T(8,128)(2,1)S(1)}, u32[]{:S(2)}, u32[]{:S(2)}) collective-permute-start(bf16[272,1024]{1,0:T(8,128)(2,1)S(1)} %multiply_convert_fusion.refs_0_.refs_5_.refs_4_), channel_id=1, source_target_pairs={{0,3},{1,0},{2,1},{3,2},{4,7},{5,4},{6,5},{7,6},{8,11},{9,8},{10,9... | collective-permute-start | bytes 1671176 | tf_op jit(solution)/shard_map/ppermute | solution.py:30
  87.1 18.2 %all-to-all-start = ((bf16[4,272,256]{2,1,0:T(8,128)(2,1)}), bf16[4,272,256]{2,1,0:T(8,128)(2,1)S(1)}, u32[]{:S(2)}, u32[]{:S(2)}) async-start(bf16[4,272,256]{2,1,0:T(8,128)(2,1)} %get-tuple-element.108), calls=%async_computation | async-start | bytes 1114112 | tf_op jit(solution)/shard_map/all_to_all | solution.py:821
  93.4 44.0 %collective-permute-start.19 = (bf16[4,3,128,768]{3,2,1,0:T(8,128)(2,1)S(1)}, bf16[4,3,128,768]{3,2,1,0:T(8,128)(2,1)}, u32[]{:S(2)}, u32[]{:S(2)}) collective-permute-start(bf16[4,3,128,768]{3,2,1,0:T(8,128)(2,1)S(1)} %pad_maximum_fusion.refs_1_), channel_id=1, source_target_pairs={{0,4},{4,0},{8,12},{12,8},{16,20},{20,16},{24,28},{28,24},{1,5},{5... | collective-permute-start | bytes 7077896 | tf_op jit(solution)/shard_map/ppermute | solution.py:141
  113.5 17.9 %collective-permute-start.14 = (bf16[272,1024]{1,0:T(8,128)(2,1)}, bf16[272,1024]{1,0:T(8,128)(2,1)}, u32[]{:S(2)}, u32[]{:S(2)}) collective-permute-start(bf16[272,1024]{1,0:T(8,128)(2,1)} %get-tuple-element.109.refs_0_), channel_id=1, source_target_pairs={{0,1},{1,2},{2,3},{3,0},{4,5},{5,6},{6,7},{7,4},{8,9},{9,10},{10,1... | collective-permute-start | bytes 1671176 | tf_op jit(solution)/shard_map/ppermute | solution.py:26
  113.8 35.3 %collective-permute-start.16 = (bf16[272,1024]{1,0:T(8,128)(2,1)}, bf16[272,1024]{1,0:T(8,128)(2,1)S(1)}, u32[]{:S(2)}, u32[]{:S(2)}) collective-permute-start(bf16[272,1024]{1,0:T(8,128)(2,1)} %get-tuple-element.109.refs_0_), channel_id=1, source_target_pairs={{0,3},{1,0},{2,1},{3,2},{4,7},{5,4},{6,5},{7,6},{8,11},{9,8},{10,9... | collective-permute-start | bytes 1671176 | tf_op jit(solution)/shard_map/ppermute | solution.py:30
  117.6 47.0 %collective-permute-start.20 = (bf16[272,1024]{1,0:T(8,128)(2,1)}, bf16[272,1024]{1,0:T(8,128)(2,1)S(1)}, u32[]{:S(2)}, u32[]{:S(2)}) collective-permute-start(bf16[272,1024]{1,0:T(8,128)(2,1)} %copy-done.24), channel_id=1, source_target_pairs={{0,1},{1,2},{2,3},{3,0},{4,5},{5,6},{6,7},{7,4},{8,9},{9,10},{10,1... | collective-permute-start | bytes 1671176 | tf_op jit(solution)/shard_map/ppermute | solution.py:26
  131.3 33.4 %collective-permute-start.15 = (bf16[272,1024]{1,0:T(8,128)(2,1)}, bf16[272,1024]{1,0:T(8,128)(2,1)S(1)}, u32[]{:S(2)}, u32[]{:S(2)}) collective-permute-start(bf16[272,1024]{1,0:T(8,128)(2,1)} %collective-permute-done.14.refs_0_.refs_1_), channel_id=1, source_target_pairs={{0,1},{1,2},{2,3},{3,0},{4,5},{5,6},{6,7},{7,4},{8,9},{9,10},{10,1... | collective-permute-start | bytes 1671176 | tf_op jit(solution)/shard_map/ppermute | solution.py:26
  191.0 21.6 %collective-permute-start.24 = (bf16[272,1024]{1,0:T(8,128)(2,1)S(1)}, bf16[272,1024]{1,0:T(8,128)(2,1)S(1)}, u32[]{:S(2)}, u32[]{:S(2)}) collective-permute-start(bf16[272,1024]{1,0:T(8,128)(2,1)S(1)} %get-tuple-element.137), channel_id=1, source_target_pairs={{0,1},{1,2},{2,3},{3,0},{4,5},{5,6},{6,7},{7,4},{8,9},{9,10},{10,1... | collective-permute-start | bytes 1671176 | tf_op jit(solution)/shard_map/ppermute | solution.py:26
  191.5 23.1 %collective-permute-start.25 = (bf16[272,1024]{1,0:T(8,128)(2,1)S(1)}, bf16[272,1024]{1,0:T(8,128)(2,1)S(1)}, u32[]{:S(2)}, u32[]{:S(2)}) collective-permute-start(bf16[272,1024]{1,0:T(8,128)(2,1)S(1)} %get-tuple-element.138), channel_id=1, source_target_pairs={{0,3},{1,0},{2,1},{3,2},{4,7},{5,4},{6,5},{7,6},{8,11},{9,8},{10,9... | collective-permute-start | bytes 1671176 | tf_op jit(solution)/shard_map/ppermute | solution.py:30
  212.5 32.8 %collective-permute-start.27 = (bf16[4,128,2304]{2,1,0:T(8,128)(2,1)}, bf16[4,128,2304]{2,1,0:T(8,128)(2,1)}, u32[]{:S(2)}, u32[]{:S(2)}) collective-permute-start(bf16[4,128,2304]{2,1,0:T(8,128)(2,1)} %get-tuple-element.146), channel_id=1, source_target_pairs={{0,4},{4,0},{8,12},{12,8},{16,20},{20,16},{24,28},{28,24},{1,5},{5... | collective-permute-start | bytes 7077896 | tf_op jit(solution)/shard_map/ppermute | solution.py:141
  215.6 15.2 %collective-permute-start.26 = (bf16[272,1024]{1,0:T(8,128)(2,1)}, bf16[272,1024]{1,0:T(8,128)(2,1)}, u32[]{:S(2)}, u32[]{:S(2)}) collective-permute-start(bf16[272,1024]{1,0:T(8,128)(2,1)} %add_convert_fusion.4), channel_id=1, source_target_pairs={{0,1},{1,2},{2,3},{3,0},{4,5},{5,6},{6,7},{7,4},{8,9},{9,10},{10,1... | collective-permute-start | bytes 1671176 | tf_op jit(solution)/shard_map/ppermute | solution.py:26
  241.8 16.7 %all-to-all-start.1 = ((bf16[4,272,256]{2,1,0:T(8,128)(2,1)}), bf16[4,272,256]{2,1,0:T(8,128)(2,1)S(1)}, u32[]{:S(2)}, u32[]{:S(2)}) async-start(bf16[4,272,256]{2,1,0:T(8,128)(2,1)} %get-tuple-element.142), calls=%async_computation.1 | async-start | bytes 1114112 | tf_op jit(solution)/shard_map/all_to_all | solution.py:973
  258.6 46.7 %all-to-all-start.2 = ((bf16[4,128,2304]{2,1,0:T(8,128)(2,1)}), bf16[4,128,2304]{2,1,0:T(8,128)(2,1)}, u32[]{:S(2)}, u32[]{:S(2)}) async-start(bf16[4,128,2304]{2,1,0:T(8,128)(2,1)} %add_convert_fusion), calls=%async_computation.2 | async-start | bytes 4718592 | tf_op jit(solution)/shard_map/all_to_all | solution.py:169
  263.1 24.7 %collective-permute-start.29 = (bf16[272,1024]{1,0:T(8,128)(2,1)}, bf16[272,1024]{1,0:T(8,128)(2,1)S(1)}, u32[]{:S(2)}, u32[]{:S(2)}) collective-permute-start(bf16[272,1024]{1,0:T(8,128)(2,1)} %copy-done.40), channel_id=1, source_target_pairs={{0,3},{1,0},{2,1},{3,2},{4,7},{5,4},{6,5},{7,6},{8,11},{9,8},{10,9... | collective-permute-start | bytes 1671176 | tf_op jit(solution)/shard_map/ppermute | solution.py:30
  264.6 24.1 %collective-permute-start.28 = (bf16[272,1024]{1,0:T(8,128)(2,1)S(1)}, bf16[272,1024]{1,0:T(8,128)(2,1)S(1)}, u32[]{:S(2)}, u32[]{:S(2)}) collective-permute-start(bf16[272,1024]{1,0:T(8,128)(2,1)S(1)} %copy-done.39), channel_id=1, source_target_pairs={{0,1},{1,2},{2,3},{3,0},{4,5},{5,6},{6,7},{7,4},{8,9},{9,10},{10,1... | collective-permute-start | bytes 1671176 | tf_op jit(solution)/shard_map/ppermute | solution.py:26
  292.5 31.4 %collective-permute-start.32 = (bf16[272,1024]{1,0:T(8,128)(2,1)}, bf16[272,1024]{1,0:T(8,128)(2,1)}, u32[]{:S(2)}, u32[]{:S(2)}) collective-permute-start(bf16[272,1024]{1,0:T(8,128)(2,1)} %get-tuple-element.158), channel_id=1, source_target_pairs={{0,1},{1,2},{2,3},{3,0},{4,5},{5,6},{6,7},{7,4},{8,9},{9,10},{10,1... | collective-permute-start | bytes 1671176 | tf_op jit(solution)/shard_map/ppermute | solution.py:26
  293.4 68.8 %collective-permute-start.37 = (bf16[272,1024]{1,0:T(8,128)(2,1)}, bf16[272,1024]{1,0:T(8,128)(2,1)}, u32[]{:S(2)}, u32[]{:S(2)}) collective-permute-start(bf16[272,1024]{1,0:T(8,128)(2,1)} %get-tuple-element.157), channel_id=1, source_target_pairs={{0,3},{1,0},{2,1},{3,2},{4,7},{5,4},{6,5},{7,6},{8,11},{9,8},{10,9... | collective-permute-start | bytes 1671176 | tf_op jit(solution)/shard_map/ppermute | solution.py:30
  302.4 18.3 %collective-permute-start.31 = (bf16[4,128,1792]{2,1,0:T(8,128)(2,1)}, bf16[4,128,1792]{2,1,0:T(8,128)(2,1)}, u32[]{:S(2)}, u32[]{:S(2)}) collective-permute-start(bf16[4,128,1792]{2,1,0:T(8,128)(2,1)} %get-tuple-element.172), channel_id=1, source_target_pairs={{0,4},{4,0},{8,12},{12,8},{16,20},{20,16},{24,28},{28,24},{1,5},{5... | collective-permute-start | bytes 5505032 | tf_op jit(solution)/shard_map/ppermute | solution.py:141
  320.7 38.5 %collective-permute-start.30 = (bf16[272,1024]{1,0:T(8,128)(2,1)}, bf16[272,1024]{1,0:T(8,128)(2,1)S(1)}, u32[]{:S(2)}, u32[]{:S(2)}) collective-permute-start(bf16[272,1024]{1,0:T(8,128)(2,1)} %add_convert_fusion.3), channel_id=1, source_target_pairs={{0,1},{1,2},{2,3},{3,0},{4,5},{5,6},{6,7},{7,4},{8,9},{9,10},{10,1... | collective-permute-start | bytes 1671176 | tf_op jit(solution)/shard_map/ppermute | solution.py:26
  323.9 27.1 %all-to-all-start.4 = ((bf16[4,128,1792]{2,1,0:T(8,128)(2,1)}), bf16[4,128,1792]{2,1,0:T(8,128)(2,1)}, u32[]{:S(2)}, u32[]{:S(2)}) async-start(bf16[4,128,1792]{2,1,0:T(8,128)(2,1)} %add_convert_fusion.1), calls=%async_computation.4 | async-start | bytes 3670016 | tf_op jit(solution)/shard_map/all_to_all | solution.py:169
  339.3 22.9 %collective-permute-start.36 = (bf16[272,1024]{1,0:T(8,128)(2,1)}, bf16[272,1024]{1,0:T(8,128)(2,1)S(1)}, u32[]{:S(2)}, u32[]{:S(2)}) collective-permute-start(bf16[272,1024]{1,0:T(8,128)(2,1)} %add_convert_fusion.2), channel_id=1, source_target_pairs={{0,1},{1,2},{2,3},{3,0},{4,5},{5,6},{6,7},{7,4},{8,9},{9,10},{10,1... | collective-permute-start | bytes 1671176 | tf_op jit(solution)/shard_map/ppermute | solution.py:26
  354.7 12.8 %collective-permute-start.38 = (bf16[128,256]{0,1:T(8,128)(2,1)S(1)}, bf16[128,256]{0,1:T(8,128)(2,1)S(1)}, u32[]{:S(2)}, u32[]{:S(2)}) collective-permute-start(bf16[128,256]{0,1:T(8,128)(2,1)S(1)} %bitcast.108), channel_id=1, source_target_pairs={{0,1},{1,2},{2,3},{3,0},{4,5},{5,6},{6,7},{7,4},{8,9},{9,10},{10,1... | collective-permute-start | bytes 196616 | tf_op jit(solution)/shard_map/ppermute | solution.py:90
  (116 other events, 983.5 us)
where the time goes:
time: 375 us; the launch traced here: 368 us
  Pallas kernels  108 us (29%)
  starting transfers between devices  82.9 us (22%)
  waiting for transfers between devices  76.4 us (20%)
  local copies, waits for them, and re-layouts  55.5 us (15%)
  other arithmetic  33.4 us (9%)
  between operations  11.1 us (3%)
    pallas_call x26, Pallas kernels, call(): pl.pallas_call(body, out_shape=outs, grid_spec=pltpu.PrefetchScalarGridSp...  108 us
    unnamed x213, local copies, waits for them, and re-layouts  42 us
    ppermute x14, waiting for transfers between devices, ring_up(): lax.ppermute(value, 'tensor', [(j, (j + 1) % size) for j in range(size)])  35.2 us
    ppermute x7, starting transfers between devices, ring_down(): lax.ppermute(value, 'tensor', [(j, (j - 1) % size) for j in range(size)])  26.5 us
    ppermute x14, starting transfers between devices, ring_up(): lax.ppermute(value, 'tensor', [(j, (j + 1) % size) for j in range(size)])  13 us
    convert_element_type x5, other arithmetic, add_low(): return (left.astype(F32) + right.astype(F32)).astype(BF)  12.7 us
    all_to_all x1, waiting for transfers between devices, on_device(): lax.all_to_all(mixed_heads, 'tensor', split_axis=0, concat_axis=0, tiled=...  9.08 us
    all_to_all x2, starting transfers between devices, dp_scatter(): lax.all_to_all(merged, 'dp', split_axis=0, concat_axis=0, tiled=True, axi...  8.94 us
  transfers between devices with their start and end apart: 46, of which 15 were waited for; matrix products, arithmetic and copies ran while one was open for 14% of the time, Pallas kernels for 26%

commit v1 on v0

--- a/solution.py
+++ b/solution.py
@@ -472,6 +472,7 @@
     length = rows.shape[0]
     for at, term in enumerate((masked, masked * hidden, scaled, scaled * hidden)):
         stats_ref[0, at : at + 1, :] = jnp.sum(term, axis=1, keepdims=True).reshape(1, length)
+    stats_ref[0, 4:8, :] = jnp.zeros((4, length), F32)
 
 
 def ffn_back_body(count, place_ref, order_ref, *refs):
@@ -877,8 +878,8 @@
             [own] * len(group)
             + [whole((rows, lanes))] * len(group)
             + [gu_block, whole(ffn_local.shape), whole(unit_row.shape)],
-            [sds(hidden_shape, F32)] * 2 + [sds((n_tp, 4, rows), F32)],
-            [hidden_block] * 2 + [ordered((4, rows))],
+            [sds(hidden_shape, F32)] * 2 + [sds((n_tp, 8, rows), F32)],
+            [hidden_block] * 2 + [ordered((8, rows))],
             (len(group),),
             scratch=[pltpu.VMEM((rows, width), BF), pltpu.VMEM((rows, lanes), F32)],
             prefetch=2,
@@ -905,7 +906,7 @@
             [hidden_block] * 2
             + [whole((rows, lanes))] * len(group)
             + [
-                ordered((rows, 4)),
+                ordered((rows, 8)),
                 gu_block,
                 whole(ffn_local.shape),
                 whole(unit_row.shape),
@@ -937,8 +938,6 @@
         (n_tp,),
         us=2.8,
     )
-
-    d_two_terms[0] = after(d_two_terms[0], *branch_parts)
 
     parity = (lax.axis_index("dp") % 2).astype(jnp.int32)[None]
     block = width // n_dp

time: 375 us -> 373 us (level)
  local copies, waits for them, and re-layouts: 55.5 us -> 50.4 us
    unnamed x213, local copies, waits for them, and re-layouts: 42 us -> 37.1 us
  transfers between devices with their start and end apart: 46 -> 46, of which waited for: 15 -> 16; matrix products, arithmetic and copies ran while one was open for 14% -> 14% of each run, Pallas kernels for 26% -> 26%
where the time goes in v1:
time: 373 us; the launch traced here: 366 us
  Pallas kernels  109 us (29%)
  starting transfers between devices  81.7 us (22%)
  waiting for transfers between devices  79.4 us (21%)
  local copies, waits for them, and re-layouts  50.4 us (14%)
  other arithmetic  33.9 us (9%)
  between operations  11.2 us (3%)
    pallas_call x26, Pallas kernels, call(): pl.pallas_call(body, out_shape=outs, grid_spec=pltpu.PrefetchScalarGridSp...  109 us
    unnamed x213, local copies, waits for them, and re-layouts  37.1 us
    ppermute x14, waiting for transfers between devices, ring_up(): lax.ppermute(value, 'tensor', [(j, (j + 1) % size) for j in range(size)])  36.3 us
    ppermute x7, starting transfers between devices, ring_down(): lax.ppermute(value, 'tensor', [(j, (j - 1) % size) for j in range(size)])  27.3 us
    convert_element_type x5, other arithmetic, add_low(): return (left.astype(F32) + right.astype(F32)).astype(BF)  13.2 us
    ppermute x14, starting transfers between devices, ring_up(): lax.ppermute(value, 'tensor', [(j, (j + 1) % size) for j in range(size)])  12.5 us
    all_to_all x1, waiting for transfers between devices, on_device(): lax.all_to_all(d_mixed_rows, 'tensor', split_axis=0, concat_axis=0, tiled...  10.1 us
    all_to_all x1, waiting for transfers between devices, on_device(): lax.all_to_all(mixed_heads, 'tensor', split_axis=0, concat_axis=0, tiled=...  9.05 us
  transfers between devices with their start and end apart: 46, of which 16 were waited for; matrix products, arithmetic and copies ran while one was open for 14% of the time, Pallas kernels for 26%

profile of v1, /device:TPU:0, one launch (start us, length us, event | category | flops | bytes accessed | tf_op | source)
XLA Modules:
  0.0 366.0 jit_solution(9226452840985835671)
XLA Ops:
  25.9 8.5 %collective-permute-start.8 = (bf16[256,128]{1,0:T(8,128)(2,1)S(1)}, bf16[256,128]{1,0:T(8,128)(2,1)S(1)}, u32[]{:S(2)}, u32[]{:S(2)}) collective-permute-start(bf16[256,128]{1,0:T(8,128)(2,1)S(1)} %copy-done.41), channel_id=1, source_target_pairs={{0,3},{1,0},{2,1},{3,2},{4,7},{5,4},{6,5},{7,6},{8,11},{9,8},{10,9... | collective-permute-start | bytes 196616 | tf_op jit(solution)/shard_map/ppermute | solution.py:30
  37.8 4.9 %collective-permute-done.7.refs_2_ = bf16[256,128]{1,0:T(8,128)(2,1)S(1)} collective-permute-done((bf16[256,128]{1,0:T(8,128)(2,1)S(1)}, bf16[256,128]{1,0:T(8,128)(2,1)S(1)}, u32[]{:S(2)}, u32[]{:S(2)}) %collective-permute-start.7) | collective-permute-done | bytes 65568 | tf_op jit(solution)/shard_map/ppermute | solution.py:26
  47.0 3.8 %collective-permute-done.9 = bf16[1,128,1024]{2,1,0:T(8,128)(2,1)} collective-permute-done((bf16[1,128,1024]{2,1,0:T(8,128)(2,1)}, bf16[1,128,1024]{2,1,0:T(8,128)(2,1)}, u32[]{:S(2)}, u32[]{:S(2)}) %collective-permute-start.9) | collective-permute-done | bytes 262176 | tf_op jit(solution)/shard_map/ppermute | solution.py:141
  63.1 4.0 %collective-permute-start.13 = (bf16[272,1024]{1,0:T(8,128)(2,1)S(1)}, bf16[272,1024]{1,0:T(8,128)(2,1)S(1)}, u32[]{:S(2)}, u32[]{:S(2)}) collective-permute-start(bf16[272,1024]{1,0:T(8,128)(2,1)S(1)} %multiply_convert_fusion.refs_0_.refs_5_.refs_4_), channel_id=1, source_target_pairs={{0,3},{1,0},{2,1},{3,2},{4,7},{5,4},{6,5},{7,6},{8,11},{9,8},{10,9... | collective-permute-start | bytes 1671176 | tf_op jit(solution)/shard_map/ppermute | solution.py:30
  69.4 10.7 %shard_map.300 = (bf16[4,272,256]{2,1,0:T(8,128)(2,1)}, f32[1,4,1088]{2,1,0:T(4,128)S(1)}) custom-call(s32[4]{0:T(128)S(1)} %and_select_fusion.2.order_ref, bf16[1088,256]{1,0:T(8,128)(2,1)S(1)} %bitcast.92, bf16[1088,256]{1,0:T(8,128)(2,1)S(1)} %bitcast.94, bf16[1088,256]{1,0:T(8,128)(2,1)S(1)} %bitcast.96, f32[1,1088]{1,0:T(1,128)S(1)} %select_n.161.bias_ref), custom_call_target="tpu_custom_call" | custom-call | flops 40000000000 | bytes 1 | tf_op jit(solution)/shard_map/pallas_call | solution.py:207
  82.4 3.8 %collective-permute-done.13.refs_2_.refs_7_ = bf16[272,1024]{1,0:T(8,128)(2,1)S(1)} collective-permute-done((bf16[272,1024]{1,0:T(8,128)(2,1)S(1)}, bf16[272,1024]{1,0:T(8,128)(2,1)S(1)}, u32[]{:S(2)}, u32[]{:S(2)}) %collective-permute-start.13) | collective-permute-done | bytes 557088 | tf_op jit(solution)/shard_map/ppermute | solution.py:30
  87.0 4.5 %all-to-all-start = ((bf16[4,272,256]{2,1,0:T(8,128)(2,1)}), bf16[4,272,256]{2,1,0:T(8,128)(2,1)S(1)}, u32[]{:S(2)}, u32[]{:S(2)}) async-start(bf16[4,272,256]{2,1,0:T(8,128)(2,1)} %get-tuple-element.107), calls=%async_computation | async-start | bytes 1114112 | tf_op jit(solution)/shard_map/all_to_all | solution.py:822
  96.2 9.0 %all-to-all-done.mixed_ref.refs_7_ = bf16[4,272,256]{2,1,0:T(8,128)(2,1)S(1)} async-done(((bf16[4,272,256]{2,1,0:T(8,128)(2,1)}), bf16[4,272,256]{2,1,0:T(8,128)(2,1)S(1)}, u32[]{:S(2)}, u32[]{:S(2)}) %all-to-all-start) | async-done | bytes 557088 | tf_op jit(solution)/shard_map/all_to_all | solution.py:822
  113.8 3.8 %collective-permute-start.16 = (bf16[272,1024]{1,0:T(8,128)(2,1)}, bf16[272,1024]{1,0:T(8,128)(2,1)S(1)}, u32[]{:S(2)}, u32[]{:S(2)}) collective-permute-start(bf16[272,1024]{1,0:T(8,128)(2,1)} %get-tuple-element.108.refs_0_), channel_id=1, source_target_pairs={{0,3},{1,0},{2,1},{3,2},{4,7},{5,4},{6,5},{7,6},{8,11},{9,8},{10,9... | collective-permute-start | bytes 1671176 | tf_op jit(solution)/shard_map/ppermute | solution.py:30
  117.6 13.7 %collective-permute-done.14.refs_0_.refs_1_ = bf16[272,1024]{1,0:T(8,128)(2,1)} collective-permute-done((bf16[272,1024]{1,0:T(8,128)(2,1)}, bf16[272,1024]{1,0:T(8,128)(2,1)}, u32[]{:S(2)}, u32[]{:S(2)}) %collective-permute-start.14) | collective-permute-done | bytes 557088 | tf_op jit(solution)/shard_map/ppermute | solution.py:26
  131.3 6.1 %collective-permute-start.15 = (bf16[272,1024]{1,0:T(8,128)(2,1)}, bf16[272,1024]{1,0:T(8,128)(2,1)S(1)}, u32[]{:S(2)}, u32[]{:S(2)}) collective-permute-start(bf16[272,1024]{1,0:T(8,128)(2,1)} %collective-permute-done.14.refs_0_.refs_1_), channel_id=1, source_target_pairs={{0,1},{1,2},{2,3},{3,0},{4,5},{5,6},{6,7},{7,4},{8,9},{9,10},{10,1... | collective-permute-start | bytes 1671176 | tf_op jit(solution)/shard_map/ppermute | solution.py:26
  137.4 4.4 %shard_map.304.refs_3_.refs_2_.refs_4_.refs_1_.refs_5_.w_ref = bf16[3,1024,768]{2,1,0:T(8,128)(2,1)S(1)} custom-call(s32[8]{0:T(128)S(1)} %broadcast_xor_fusion.refs_0_, bf16[4,3,128,768]{3,2,1,0:T(8,128)(2,1)S(1)} %pad_maximum_fusion.refs_1_, bf16[4,3,128,768]{3,2,1,0:T(8,128)(2,1)} %collective-permute-done.19.refs_2_), custom_call_target="tpu_custom_call" | custom-call | flops 17999998976 | bytes 1 | tf_op jit(solution)/shard_map/pallas_call | solution.py:207
  144.0 5.0 %shard_map.306 = (f32[4,272,768]{2,1,0:T(8,128)S(1)}, f32[4,272,768]{2,1,0:T(8,128)S(1)}, f32[4,8,272]{2,1,0:T(8,128)S(1)}) custom-call(s32[1]{0:T(128)} %constant.167.clone.place_ref, s32[4]{0:T(128)S(1)} %and_select_fusion.2.order_ref, bf16[272,1024]{1,0:T(8,128)(2,1)} %get-tuple-element.108.refs_0_, f32[272,768]{1,0:T(8,128)S(1)} %get-tuple-element.114.refs_1_.refs_2_, ...), custom_call_target="tpu_custom_call" | custom-call | flops 13600000000 | bytes 1 | tf_op jit(solution)/shard_map/pallas_call | solution.py:207
  149.1 5.4 %shard_map.307 = (f32[4,272,768]{2,1,0:T(8,128)S(1)}, f32[4,272,768]{2,1,0:T(8,128)S(1)}, f32[4,8,272]{2,1,0:T(8,128)S(1)}) custom-call(s32[2]{0:T(128)S(1)} %copy-done.54, s32[4]{0:T(128)S(1)} %and_select_fusion.2.order_ref, bf16[272,1024]{1,0:T(8,128)(2,1)} %collective-permute-done.14.refs_0_.refs_1_, ...), custom_call_target="tpu_custom_call", output_to_operand_aliasing={{0}: (9, {}), {1}: (10, {}), {2}: (11, {})} | custom-call | flops 22400000000 | bytes 1 | tf_op jit(solution)/shard_map/pallas_call | solution.py:207
  154.6 9.7 %collective-permute-done.15.refs_0_.refs_2_ = bf16[272,1024]{1,0:T(8,128)(2,1)S(1)} collective-permute-done((bf16[272,1024]{1,0:T(8,128)(2,1)}, bf16[272,1024]{1,0:T(8,128)(2,1)S(1)}, u32[]{:S(2)}, u32[]{:S(2)}) %collective-permute-start.15) | collective-permute-done | bytes 557088 | tf_op jit(solution)/shard_map/ppermute | solution.py:26
  165.3 3.7 %shard_map.309 = (f32[4,272,768]{2,1,0:T(8,128)S(1)}, f32[4,272,768]{2,1,0:T(8,128)S(1)}, f32[4,8,272]{2,1,0:T(8,128)S(1)}) custom-call(s32[1]{0:T(128)} %constant.169.clone.place_ref, s32[4]{0:T(128)S(1)} %and_select_fusion.2.order_ref, ...), custom_call_target="tpu_custom_call", output_to_operand_aliasing={{0}: (7, {}), {1}: (8, {}), {2}: (9, {})} | custom-call | flops 13600000000 | bytes 1 | tf_op jit(solution)/shard_map/pallas_call | solution.py:207
  183.2 8.5 %shard_map.310 = (bf16[4,272,768]{2,1,0:T(8,128)(2,1)S(1)}, bf16[4,272,768]{2,1,0:T(8,128)(2,1)S(1)}, bf16[4,272,768]{2,1,0:T(8,128)(2,1)S(1)}, f32[4,768]{1,0:T...) custom-call(s32[2]{0:T(128)S(1)} %copy-done.52, s32[4]{0:T(128)S(1)} %and_select_fusion.2.order_ref, ...), custom_call_target="tpu_custom_call" | custom-call | flops 29600000000 | bytes 1 | tf_op jit(solution)/shard_map/pallas_call | solution.py:207
  196.0 7.8 %shard_map.311 = (bf16[4,272,768]{2,1,0:T(8,128)(2,1)S(1)}, bf16[4,272,768]{2,1,0:T(8,128)(2,1)S(1)}, bf16[4,272,768]{2,1,0:T(8,128)(2,1)S(1)}, f32[4,768]{1,0:T...) custom-call(s32[2]{0:T(128)S(1)} %iota_multiply_fusion.place_ref, ...), custom_call_target="tpu_custom_call", output_to_operand_aliasing={{0}: (10, {}), {1}: (11, {}), {2}: (12, {})} | custom-call | flops 29600000000 | bytes 1 | tf_op jit(solution)/shard_map/pallas_call | solution.py:207
  203.8 9.7 %shard_map.314 = (bf16[4,128,2304]{2,1,0:T(8,128)(2,1)}, bf16[4,128,2304]{2,1,0:T(8,128)(2,1)}) custom-call(s32[1]{0:T(128)} %bitcast.23.parity_ref, bf16[272,1024]{1,0:T(8,128)(2,1)} %get-tuple-element.108.refs_0_, bf16[272,1024]{1,0:T(8,128)(2,1)} %collective-permute-done.14.refs_0_.refs_1_, bf16[272,1024]{1,0:T(8,128)(2,1)S(1)} %copy-done.35, ...), custom_call_target="tpu_custom_call" | custom-call | flops 36864000000 | bytes 1 | tf_op jit(solution)/shard_map/pallas_call | solution.py:207
  225.5 7.3 %collective-permute-done.26.refs_1_ = bf16[272,1024]{1,0:T(8,128)(2,1)S(1)} collective-permute-done((bf16[272,1024]{1,0:T(8,128)(2,1)S(1)}, bf16[272,1024]{1,0:T(8,128)(2,1)S(1)}, u32[]{:S(2)}, u32[]{:S(2)}) %collective-permute-start.26) | collective-permute-done | bytes 557088 | tf_op jit(solution)/shard_map/ppermute | solution.py:26
  241.3 4.3 %add_convert_fusion = bf16[4,128,2304]{2,1,0:T(8,128)(2,1)} fusion(bf16[4,128,2304]{2,1,0:T(8,128)(2,1)} %collective-permute-done.27, bf16[4,128,2304]{2,1,0:T(8,128)(2,1)} %get-tuple-element.140), kind=kLoop, calls=%fused_computation.1 | loop fusion | flops 4718592 | bytes 7077888 | tf_op jit(solution)/shard_map/convert_element_type | solution.py:96
  245.7 10.1 %all-to-all-done.1.dmix_ref = bf16[4,272,256]{2,1,0:T(8,128)(2,1)S(1)} async-done(((bf16[4,272,256]{2,1,0:T(8,128)(2,1)}), bf16[4,272,256]{2,1,0:T(8,128)(2,1)S(1)}, u32[]{:S(2)}, u32[]{:S(2)}) %all-to-all-start.1) | async-done | bytes 557088 | tf_op jit(solution)/shard_map/all_to_all | solution.py:972
  255.8 4.5 %all-to-all-start.2 = ((bf16[4,128,2304]{2,1,0:T(8,128)(2,1)}), bf16[4,128,2304]{2,1,0:T(8,128)(2,1)}, u32[]{:S(2)}, u32[]{:S(2)}) async-start(bf16[4,128,2304]{2,1,0:T(8,128)(2,1)} %add_convert_fusion), calls=%async_computation.2 | async-start | bytes 4718592 | tf_op jit(solution)/shard_map/all_to_all | solution.py:169
  265.7 18.8 %shard_map.315 = (bf16[1088,256]{1,0:T(8,128)(2,1)S(1)}, bf16[1088,256]{1,0:T(8,128)(2,1)S(1)}, bf16[1088,256]{1,0:T(8,128)(2,1)S(1)}, f32[8,256]{1,0:T(8,128)S(1)}) custom-call(s32[4]{0:T(128)S(1)} %and_select_fusion.2.order_ref, bf16[1088,256]{1,0:T(8,128)(2,1)S(1)} %bitcast.93, bf16[4,272,256]{2,1,0:T(8,128)(2,1)S(1)} %all-to-all-done.1.dmix_ref, ...), custom_call_target="tpu_custom_call" | custom-call | flops 96000000000 | bytes 1 | tf_op jit(solution)/shard_map/pallas_call | solution.py:207
  290.8 3.8 %collective-permute-start.37 = (bf16[272,1024]{1,0:T(8,128)(2,1)}, bf16[272,1024]{1,0:T(8,128)(2,1)}, u32[]{:S(2)}, u32[]{:S(2)}) collective-permute-start(bf16[272,1024]{1,0:T(8,128)(2,1)} %get-tuple-element.154), channel_id=1, source_target_pairs={{0,3},{1,0},{2,1},{3,2},{4,7},{5,4},{6,5},{7,6},{8,11},{9,8},{10,9... | collective-permute-start | bytes 1671176 | tf_op jit(solution)/shard_map/ppermute | solution.py:30
  294.6 6.1 %shard_map.317 = (bf16[4,128,1792]{2,1,0:T(8,128)(2,1)S(1)}, bf16[4,128,1792]{2,1,0:T(8,128)(2,1)}, f32[4,1,256]{2,1,0:T(1,128)S(1)}) custom-call(s32[1]{0:T(128)} %bitcast.23.parity_ref, bf16[272,1024]{1,0:T(8,128)(2,1)} %shard_map.295.refs_0_, bf16[272,1024]{1,0:T(8,128)(2,1)S(1)} %copy-done.21, bf16[272,1024]{1,0:T(8,128)(2,1)S(1)} %copy-done.23, ...), custom_call_target="tpu_custom_call" | custom-call | flops 28672000000 | bytes 1 | tf_op jit(solution)/shard_map/pallas_call | solution.py:207
  304.3 3.9 %all-to-all-start.3 = ((f32[8,96,128]{2,1,0:T(8,128)}), f32[8,96,128]{2,1,0:T(8,128)S(1)}, u32[]{:S(2)}, u32[]{:S(2)}) async-start(f32[8,96,128]{2,1,0:T(8,128)} %broadcast_in_dim.61), calls=%async_computation.3 | async-start | bytes 786432 | tf_op jit(solution)/shard_map/all_to_all | solution.py:180
  321.9 4.4 %all-to-all-start.4 = ((bf16[4,128,1792]{2,1,0:T(8,128)(2,1)}), bf16[4,128,1792]{2,1,0:T(8,128)(2,1)}, u32[]{:S(2)}, u32[]{:S(2)}) async-start(bf16[4,128,1792]{2,1,0:T(8,128)(2,1)} %add_convert_fusion.1), calls=%async_computation.4 | async-start | bytes 3670016 | tf_op jit(solution)/shard_map/all_to_all | solution.py:169
  328.4 4.4 %collective-permute-start.33 = (f32[96,128]{1,0:T(8,128)S(1)}, f32[96,128]{1,0:T(8,128)S(1)}, u32[]{:S(2)}, u32[]{:S(2)}) collective-permute-start(f32[96,128]{1,0:T(8,128)S(1)} %reduce_sum.57), channel_id=1, source_target_pairs={{0,2},{1,3},{2,0},{3,1},{4,6},{5,7},{6,4},{7,5},{8,10},{9,11},{10,... | collective-permute-start | bytes 147464 | tf_op jit(solution)/shard_map/ppermute | solution.py:70
  333.3 4.1 %collective-permute-done.34 = f32[96,128]{1,0:T(8,128)S(1)} collective-permute-done((f32[96,128]{1,0:T(8,128)S(1)}, f32[96,128]{1,0:T(8,128)S(1)}, u32[]{:S(2)}, u32[]{:S(2)}) %collective-permute-start.34) | collective-permute-done | bytes 49184 | tf_op jit(solution)/shard_map/ppermute | solution.py:70
  341.6 7.3 %all-to-all-done.4 = bf16[4,128,1792]{2,1,0:T(8,128)(2,1)} async-done(((bf16[4,128,1792]{2,1,0:T(8,128)(2,1)}), bf16[4,128,1792]{2,1,0:T(8,128)(2,1)}, u32[]{:S(2)}, u32[]{:S(2)}) %all-to-all-start.4) | async-done | bytes 1835040 | tf_op jit(solution)/shard_map/all_to_all | solution.py:169
  352.9 4.2 %collective-permute-start.39 = (bf16[128,256]{0,1:T(8,128)(2,1)S(1)}, bf16[128,256]{0,1:T(8,128)(2,1)S(1)}, u32[]{:S(2)}, u32[]{:S(2)}) collective-permute-start(bf16[128,256]{0,1:T(8,128)(2,1)S(1)} %bitcast.109), channel_id=1, source_target_pairs={{0,2},{1,3},{2,0},{3,1},{4,6},{5,7},{6,4},{7,5},{8,10},{9,11},{10,... | collective-permute-start | bytes 196616 | tf_op jit(solution)/shard_map/ppermute | solution.py:90
  (417 shorter events, 144.5 us)
Async XLA Ops:
  3.7 22.1 %collective-permute-start = (bf16[272,1024]{1,0:T(8,128)(2,1)}, bf16[272,1024]{1,0:T(8,128)(2,1)S(1)}, u32[]{:S(2)}, u32[]{:S(2)}) collective-permute-start(bf16[272,1024]{1,0:T(8,128)(2,1)} %shard_map.295.refs_0_), channel_id=1, source_target_pairs={{0,1},{1,2},{2,3},{3,0},{4,5},{5,6},{6,7},{7,4},{8,9},{9,10},{10,1... | collective-permute-start | bytes 1671176 | tf_op jit(solution)/shard_map/ppermute | solution.py:26
  6.7 53.0 %collective-permute-start.2 = (bf16[272,1024]{1,0:T(8,128)(2,1)}, bf16[272,1024]{1,0:T(8,128)(2,1)}, u32[]{:S(2)}, u32[]{:S(2)}) collective-permute-start(bf16[272,1024]{1,0:T(8,128)(2,1)} %shard_map.295.refs_0_), channel_id=1, source_target_pairs={{0,3},{1,0},{2,1},{3,2},{4,7},{5,4},{6,5},{7,6},{8,11},{9,8},{10,9... | collective-permute-start | bytes 1671176 | tf_op jit(solution)/shard_map/ppermute | solution.py:30
  8.7 13.8 %collective-permute-start.3 = (bf16[1,3,128,256]{3,2,1,0:T(8,128)(2,1)S(1)}, bf16[1,3,128,256]{3,2,1,0:T(8,128)(2,1)S(1)}, u32[]{:S(2)}, u32[]{:S(2)}) collective-permute-start(bf16[1,3,128,256]{3,2,1,0:T(8,128)(2,1)S(1)} %bitcast.104), channel_id=1, source_target_pairs={{0,8},{4,12},{8,0},{12,4},{16,24},{20,28},{24,16},{28,20},{1,9},{5... | collective-permute-start | bytes 589832 | tf_op jit(solution)/shard_map/ppermute | solution.py:141
  22.6 14.0 %collective-permute-start.4 = (bf16[2,3,128,256]{3,2,1,0:T(8,128)(2,1)S(1)}, bf16[2,3,128,256]{3,2,1,0:T(8,128)(2,1)}, u32[]{:S(2)}, u32[]{:S(2)}) collective-permute-start(bf16[2,3,128,256]{3,2,1,0:T(8,128)(2,1)S(1)} %pad_maximum_fusion.6), channel_id=1, source_target_pairs={{0,16},{4,20},{8,24},{12,28},{16,0},{20,4},{24,8},{28,12},{1,17},{... | collective-permute-start | bytes 1179656 | tf_op jit(solution)/shard_map/ppermute | solution.py:141
  34.4 19.1 %collective-permute-start.17 = (bf16[1,3,128,768]{3,2,1,0:T(8,128)(2,1)}, bf16[1,3,128,768]{3,2,1,0:T(8,128)(2,1)}, u32[]{:S(2)}, u32[]{:S(2)}) collective-permute-start(bf16[1,3,128,768]{3,2,1,0:T(8,128)(2,1)} %bitcast.21), channel_id=1, source_target_pairs={{0,8},{4,12},{8,0},{12,4},{16,24},{20,28},{24,16},{28,20},{1,9},{5... | collective-permute-start | bytes 1769480 | tf_op jit(solution)/shard_map/ppermute | solution.py:141
  37.7 18.7 %collective-permute-start.5 = (bf16[4,3,128,256]{3,2,1,0:T(8,128)(2,1)S(1)}, bf16[4,3,128,256]{3,2,1,0:T(8,128)(2,1)S(1)}, u32[]{:S(2)}, u32[]{:S(2)}) collective-permute-start(bf16[4,3,128,256]{3,2,1,0:T(8,128)(2,1)S(1)} %pad_maximum_fusion.3.refs_1_), channel_id=1, source_target_pairs={{0,4},{4,0},{8,12},{12,8},{16,20},{20,16},{24,28},{28,24},{1,5},{5... | collective-permute-start | bytes 2359304 | tf_op jit(solution)/shard_map/ppermute | solution.py:141
  47.0 16.0 %collective-permute-start.1 = (bf16[272,1024]{1,0:T(8,128)(2,1)}, bf16[272,1024]{1,0:T(8,128)(2,1)S(1)}, u32[]{:S(2)}, u32[]{:S(2)}) collective-permute-start(bf16[272,1024]{1,0:T(8,128)(2,1)} %copy-done.19), channel_id=1, source_target_pairs={{0,1},{1,2},{2,3},{3,0},{4,5},{5,6},{6,7},{7,4},{8,9},{9,10},{10,1... | collective-permute-start | bytes 1671176 | tf_op jit(solution)/shard_map/ppermute | solution.py:26
  51.9 15.9 %collective-permute-start.10 = (bf16[2,128,1024]{2,1,0:T(8,128)(2,1)S(1)}, bf16[2,128,1024]{2,1,0:T(8,128)(2,1)S(1)}, u32[]{:S(2)}, u32[]{:S(2)}) collective-permute-start(bf16[2,128,1024]{2,1,0:T(8,128)(2,1)S(1)} %pad_maximum_fusion.5), channel_id=1, source_target_pairs={{0,16},{4,20},{8,24},{12,28},{16,0},{20,4},{24,8},{28,12},{1,17},{... | collective-permute-start | bytes 1572872 | tf_op jit(solution)/shard_map/ppermute | solution.py:141
  55.9 35.7 %collective-permute-start.18 = (bf16[2,3,128,768]{3,2,1,0:T(8,128)(2,1)}, bf16[2,3,128,768]{3,2,1,0:T(8,128)(2,1)}, u32[]{:S(2)}, u32[]{:S(2)}) collective-permute-start(bf16[2,3,128,768]{3,2,1,0:T(8,128)(2,1)} %pad_maximum_fusion.1), channel_id=1, source_target_pairs={{0,16},{4,20},{8,24},{12,28},{16,0},{20,4},{24,8},{28,12},{1,17},{... | collective-permute-start | bytes 3538952 | tf_op jit(solution)/shard_map/ppermute | solution.py:141
  63.0 19.4 %collective-permute-start.12 = (bf16[272,1024]{1,0:T(8,128)(2,1)S(1)}, bf16[272,1024]{1,0:T(8,128)(2,1)S(1)}, u32[]{:S(2)}, u32[]{:S(2)}) collective-permute-start(bf16[272,1024]{1,0:T(8,128)(2,1)S(1)} %multiply_convert_fusion.refs_0_.refs_5_.refs_4_), channel_id=1, source_target_pairs={{0,1},{1,2},{2,3},{3,0},{4,5},{5,6},{6,7},{7,4},{8,9},{9,10},{10,1... | collective-permute-start | bytes 1671176 | tf_op jit(solution)/shard_map/ppermute | solution.py:26
  63.1 23.1 %collective-permute-start.13 = (bf16[272,1024]{1,0:T(8,128)(2,1)S(1)}, bf16[272,1024]{1,0:T(8,128)(2,1)S(1)}, u32[]{:S(2)}, u32[]{:S(2)}) collective-permute-start(bf16[272,1024]{1,0:T(8,128)(2,1)S(1)} %multiply_convert_fusion.refs_0_.refs_5_.refs_4_), channel_id=1, source_target_pairs={{0,3},{1,0},{2,1},{3,2},{4,7},{5,4},{6,5},{7,6},{8,11},{9,8},{10,9... | collective-permute-start | bytes 1671176 | tf_op jit(solution)/shard_map/ppermute | solution.py:30
  87.0 18.2 %all-to-all-start = ((bf16[4,272,256]{2,1,0:T(8,128)(2,1)}), bf16[4,272,256]{2,1,0:T(8,128)(2,1)S(1)}, u32[]{:S(2)}, u32[]{:S(2)}) async-start(bf16[4,272,256]{2,1,0:T(8,128)(2,1)} %get-tuple-element.107), calls=%async_computation | async-start | bytes 1114112 | tf_op jit(solution)/shard_map/all_to_all | solution.py:822
  93.4 43.9 %collective-permute-start.19 = (bf16[4,3,128,768]{3,2,1,0:T(8,128)(2,1)S(1)}, bf16[4,3,128,768]{3,2,1,0:T(8,128)(2,1)}, u32[]{:S(2)}, u32[]{:S(2)}) collective-permute-start(bf16[4,3,128,768]{3,2,1,0:T(8,128)(2,1)S(1)} %pad_maximum_fusion.refs_1_), channel_id=1, source_target_pairs={{0,4},{4,0},{8,12},{12,8},{16,20},{20,16},{24,28},{28,24},{1,5},{5... | collective-permute-start | bytes 7077896 | tf_op jit(solution)/shard_map/ppermute | solution.py:141
  113.4 17.9 %collective-permute-start.14 = (bf16[272,1024]{1,0:T(8,128)(2,1)}, bf16[272,1024]{1,0:T(8,128)(2,1)}, u32[]{:S(2)}, u32[]{:S(2)}) collective-permute-start(bf16[272,1024]{1,0:T(8,128)(2,1)} %get-tuple-element.108.refs_0_), channel_id=1, source_target_pairs={{0,1},{1,2},{2,3},{3,0},{4,5},{5,6},{6,7},{7,4},{8,9},{9,10},{10,1... | collective-permute-start | bytes 1671176 | tf_op jit(solution)/shard_map/ppermute | solution.py:26
  113.8 35.3 %collective-permute-start.16 = (bf16[272,1024]{1,0:T(8,128)(2,1)}, bf16[272,1024]{1,0:T(8,128)(2,1)S(1)}, u32[]{:S(2)}, u32[]{:S(2)}) collective-permute-start(bf16[272,1024]{1,0:T(8,128)(2,1)} %get-tuple-element.108.refs_0_), channel_id=1, source_target_pairs={{0,3},{1,0},{2,1},{3,2},{4,7},{5,4},{6,5},{7,6},{8,11},{9,8},{10,9... | collective-permute-start | bytes 1671176 | tf_op jit(solution)/shard_map/ppermute | solution.py:30
  117.6 46.7 %collective-permute-start.20 = (bf16[272,1024]{1,0:T(8,128)(2,1)}, bf16[272,1024]{1,0:T(8,128)(2,1)S(1)}, u32[]{:S(2)}, u32[]{:S(2)}) collective-permute-start(bf16[272,1024]{1,0:T(8,128)(2,1)} %copy-done.24), channel_id=1, source_target_pairs={{0,1},{1,2},{2,3},{3,0},{4,5},{5,6},{6,7},{7,4},{8,9},{9,10},{10,1... | collective-permute-start | bytes 1671176 | tf_op jit(solution)/shard_map/ppermute | solution.py:26
  131.3 33.0 %collective-permute-start.15 = (bf16[272,1024]{1,0:T(8,128)(2,1)}, bf16[272,1024]{1,0:T(8,128)(2,1)S(1)}, u32[]{:S(2)}, u32[]{:S(2)}) collective-permute-start(bf16[272,1024]{1,0:T(8,128)(2,1)} %collective-permute-done.14.refs_0_.refs_1_), channel_id=1, source_target_pairs={{0,1},{1,2},{2,3},{3,0},{4,5},{5,6},{6,7},{7,4},{8,9},{9,10},{10,1... | collective-permute-start | bytes 1671176 | tf_op jit(solution)/shard_map/ppermute | solution.py:26
  191.8 22.6 %collective-permute-start.24 = (bf16[272,1024]{1,0:T(8,128)(2,1)}, bf16[272,1024]{1,0:T(8,128)(2,1)}, u32[]{:S(2)}, u32[]{:S(2)}) collective-permute-start(bf16[272,1024]{1,0:T(8,128)(2,1)} %get-tuple-element.132), channel_id=1, source_target_pairs={{0,1},{1,2},{2,3},{3,0},{4,5},{5,6},{6,7},{7,4},{8,9},{9,10},{10,1... | collective-permute-start | bytes 1671176 | tf_op jit(solution)/shard_map/ppermute | solution.py:26
  192.3 22.8 %collective-permute-start.25 = (bf16[272,1024]{1,0:T(8,128)(2,1)}, bf16[272,1024]{1,0:T(8,128)(2,1)S(1)}, u32[]{:S(2)}, u32[]{:S(2)}) collective-permute-start(bf16[272,1024]{1,0:T(8,128)(2,1)} %get-tuple-element.133), channel_id=1, source_target_pairs={{0,3},{1,0},{2,1},{3,2},{4,7},{5,4},{6,5},{7,6},{8,11},{9,8},{10,9... | collective-permute-start | bytes 1671176 | tf_op jit(solution)/shard_map/ppermute | solution.py:30
  213.6 27.7 %collective-permute-start.27 = (bf16[4,128,2304]{2,1,0:T(8,128)(2,1)}, bf16[4,128,2304]{2,1,0:T(8,128)(2,1)}, u32[]{:S(2)}, u32[]{:S(2)}) collective-permute-start(bf16[4,128,2304]{2,1,0:T(8,128)(2,1)} %get-tuple-element.141), channel_id=1, source_target_pairs={{0,4},{4,0},{8,12},{12,8},{16,20},{20,16},{24,28},{28,24},{1,5},{5... | collective-permute-start | bytes 7077896 | tf_op jit(solution)/shard_map/ppermute | solution.py:141
  216.6 16.2 %collective-permute-start.26 = (bf16[272,1024]{1,0:T(8,128)(2,1)S(1)}, bf16[272,1024]{1,0:T(8,128)(2,1)S(1)}, u32[]{:S(2)}, u32[]{:S(2)}) collective-permute-start(bf16[272,1024]{1,0:T(8,128)(2,1)S(1)} %add_convert_fusion.4), channel_id=1, source_target_pairs={{0,1},{1,2},{2,3},{3,0},{4,5},{5,6},{6,7},{7,4},{8,9},{9,10},{10,1... | collective-permute-start | bytes 1671176 | tf_op jit(solution)/shard_map/ppermute | solution.py:26
  237.8 18.0 %all-to-all-start.1 = ((bf16[4,272,256]{2,1,0:T(8,128)(2,1)}), bf16[4,272,256]{2,1,0:T(8,128)(2,1)S(1)}, u32[]{:S(2)}, u32[]{:S(2)}) async-start(bf16[4,272,256]{2,1,0:T(8,128)(2,1)} %get-tuple-element.137), calls=%async_computation.1 | async-start | bytes 1114112 | tf_op jit(solution)/shard_map/all_to_all | solution.py:972
  255.8 47.7 %all-to-all-start.2 = ((bf16[4,128,2304]{2,1,0:T(8,128)(2,1)}), bf16[4,128,2304]{2,1,0:T(8,128)(2,1)}, u32[]{:S(2)}, u32[]{:S(2)}) async-start(bf16[4,128,2304]{2,1,0:T(8,128)(2,1)} %add_convert_fusion), calls=%async_computation.2 | async-start | bytes 4718592 | tf_op jit(solution)/shard_map/all_to_all | solution.py:169
  260.3 25.8 %collective-permute-start.29 = (bf16[272,1024]{1,0:T(8,128)(2,1)}, bf16[272,1024]{1,0:T(8,128)(2,1)S(1)}, u32[]{:S(2)}, u32[]{:S(2)}) collective-permute-start(bf16[272,1024]{1,0:T(8,128)(2,1)} %copy-done.38), channel_id=1, source_target_pairs={{0,3},{1,0},{2,1},{3,2},{4,7},{5,4},{6,5},{7,6},{8,11},{9,8},{10,9... | collective-permute-start | bytes 1671176 | tf_op jit(solution)/shard_map/ppermute | solution.py:30
  261.8 25.1 %collective-permute-start.28 = (bf16[272,1024]{1,0:T(8,128)(2,1)S(1)}, bf16[272,1024]{1,0:T(8,128)(2,1)S(1)}, u32[]{:S(2)}, u32[]{:S(2)}) collective-permute-start(bf16[272,1024]{1,0:T(8,128)(2,1)S(1)} %get-tuple-element.145), channel_id=1, source_target_pairs={{0,1},{1,2},{2,3},{3,0},{4,5},{5,6},{6,7},{7,4},{8,9},{9,10},{10,1... | collective-permute-start | bytes 1671176 | tf_op jit(solution)/shard_map/ppermute | solution.py:26
  290.8 31.2 %collective-permute-start.32 = (bf16[272,1024]{1,0:T(8,128)(2,1)}, bf16[272,1024]{1,0:T(8,128)(2,1)}, u32[]{:S(2)}, u32[]{:S(2)}) collective-permute-start(bf16[272,1024]{1,0:T(8,128)(2,1)} %get-tuple-element.155), channel_id=1, source_target_pairs={{0,1},{1,2},{2,3},{3,0},{4,5},{5,6},{6,7},{7,4},{8,9},{9,10},{10,1... | collective-permute-start | bytes 1671176 | tf_op jit(solution)/shard_map/ppermute | solution.py:26
  290.8 69.1 %collective-permute-start.37 = (bf16[272,1024]{1,0:T(8,128)(2,1)}, bf16[272,1024]{1,0:T(8,128)(2,1)}, u32[]{:S(2)}, u32[]{:S(2)}) collective-permute-start(bf16[272,1024]{1,0:T(8,128)(2,1)} %get-tuple-element.154), channel_id=1, source_target_pairs={{0,3},{1,0},{2,1},{3,2},{4,7},{5,4},{6,5},{7,6},{8,11},{9,8},{10,9... | collective-permute-start | bytes 1671176 | tf_op jit(solution)/shard_map/ppermute | solution.py:30
  300.7 18.0 %collective-permute-start.31 = (bf16[4,128,1792]{2,1,0:T(8,128)(2,1)}, bf16[4,128,1792]{2,1,0:T(8,128)(2,1)}, u32[]{:S(2)}, u32[]{:S(2)}) collective-permute-start(bf16[4,128,1792]{2,1,0:T(8,128)(2,1)} %get-tuple-element.170), channel_id=1, source_target_pairs={{0,4},{4,0},{8,12},{12,8},{16,20},{20,16},{24,28},{28,24},{1,5},{5... | collective-permute-start | bytes 5505032 | tf_op jit(solution)/shard_map/ppermute | solution.py:141
  318.7 38.5 %collective-permute-start.30 = (bf16[272,1024]{1,0:T(8,128)(2,1)}, bf16[272,1024]{1,0:T(8,128)(2,1)S(1)}, u32[]{:S(2)}, u32[]{:S(2)}) collective-permute-start(bf16[272,1024]{1,0:T(8,128)(2,1)} %add_convert_fusion.3), channel_id=1, source_target_pairs={{0,1},{1,2},{2,3},{3,0},{4,5},{5,6},{6,7},{7,4},{8,9},{9,10},{10,1... | collective-permute-start | bytes 1671176 | tf_op jit(solution)/shard_map/ppermute | solution.py:26
  321.9 27.0 %all-to-all-start.4 = ((bf16[4,128,1792]{2,1,0:T(8,128)(2,1)}), bf16[4,128,1792]{2,1,0:T(8,128)(2,1)}, u32[]{:S(2)}, u32[]{:S(2)}) async-start(bf16[4,128,1792]{2,1,0:T(8,128)(2,1)} %add_convert_fusion.1), calls=%async_computation.4 | async-start | bytes 3670016 | tf_op jit(solution)/shard_map/all_to_all | solution.py:169
  337.3 22.5 %collective-permute-start.36 = (bf16[272,1024]{1,0:T(8,128)(2,1)}, bf16[272,1024]{1,0:T(8,128)(2,1)S(1)}, u32[]{:S(2)}, u32[]{:S(2)}) collective-permute-start(bf16[272,1024]{1,0:T(8,128)(2,1)} %add_convert_fusion.2), channel_id=1, source_target_pairs={{0,1},{1,2},{2,3},{3,0},{4,5},{5,6},{6,7},{7,4},{8,9},{9,10},{10,1... | collective-permute-start | bytes 1671176 | tf_op jit(solution)/shard_map/ppermute | solution.py:26
  352.7 12.4 %collective-permute-start.38 = (bf16[128,256]{0,1:T(8,128)(2,1)S(1)}, bf16[128,256]{0,1:T(8,128)(2,1)S(1)}, u32[]{:S(2)}, u32[]{:S(2)}) collective-permute-start(bf16[128,256]{0,1:T(8,128)(2,1)S(1)} %bitcast.108), channel_id=1, source_target_pairs={{0,1},{1,2},{2,3},{3,0},{4,5},{5,6},{6,7},{7,4},{8,9},{9,10},{10,1... | collective-permute-start | bytes 196616 | tf_op jit(solution)/shard_map/ppermute | solution.py:90
  (116 other events, 1025.0 us)
